TPU v7x, 32 devices: a whole 2x2x4 slice. The times are simulated.
32 devices in a mesh: fsdp: 16 (over z, y, core), sp: 2 (over x).
Axes of the slice: x: 2, y: 2, z: 4, core: 2. Of those that a mesh axis runs over, the one named last changes fastest.
Arguments:
- tokens: bfloat16 [4096, 1536], P(('fsdp', 'sp')), may hold values from -6 to 6
- cotangent: bfloat16 [4096, 1536], P(('fsdp', 'sp')), may hold values from -6 to 6
- routes: int32 [4096, 4], P(('fsdp', 'sp')), may hold values from 0 to 31, all different within a row; in each aligned block of 128 rows (0 to 127, 128 to 255, ...) at most 32 rows name the same one
- attn_gain: bfloat16 [1536], P('fsdp'), may hold values from 0.25 to 1.75
- query_weight: bfloat16 [1536, 1536], P('fsdp'), may hold values from -0.15625 to 0.15625
- key_matrix: bfloat16 [1536, 256], P('fsdp'), may hold values from -0.15625 to 0.15625
- value_matrix: bfloat16 [1536, 256], P('fsdp'), may hold values from -0.15625 to 0.15625
- output_weight: bfloat16 [1536, 1536], P('fsdp'), may hold values from -2.5 to 2.5
- moe_gain: bfloat16 [1536], P('fsdp'), may hold values from 0.25 to 1.75
- router_weight: bfloat16 [1536, 32], P('fsdp'), may hold values from -0.078125 to 0.078125
- gate_weight: bfloat16 [1536, 24576], P(None, 'fsdp'), may hold values from -0.15625 to 0.15625
- up_weight: bfloat16 [1536, 24576], P(None, 'fsdp'), may hold values from -0.15625 to 0.15625
- down_weight: bfloat16 [24576, 1536], P('fsdp'), may hold values from -0.4375 to 0.4375
Outputs:
- output: bfloat16 [4096, 1536], P(('fsdp', 'sp'))
- input_grad: bfloat16 [4096, 1536], P(('fsdp', 'sp'))
- query_grad: float32 [1536, 1536], P('fsdp')
- key_grad: float32 [1536, 256], P('fsdp')
- value_grad: float32 [1536, 256], P('fsdp')
- output_grad: float32 [1536, 1536], P('fsdp')
- router_grad: float32 [1536, 32], P('fsdp')
- gate_grad: float32 [1536, 24576], P(None, 'fsdp')
- up_grad: float32 [1536, 24576], P(None, 'fsdp')
- down_grad: float32 [24576, 1536], P('fsdp')
- attn_gain_grad: float32 [1536], P('fsdp')
- moe_gain_grad: float32 [1536], P('fsdp')
Inputs may be any that keep to these rules, and one draw needn't show every extreme that they name: `routes`: each row names 4 different experts. Among the rows of one device no expert is named more than 32 times, a bound that some block reaches.
All inputs are finite; a program needn't handle non-finite values.
Results may differ from a plain program's by a relative error of at most 0.019.
Values may be sent and summed in bfloat16 or wider, within the bound.
No kernel may reach another device: no remote copies, remote signals or barrier semaphores. Data moves between devices by JAX's collectives and lax.ppermute only.
A program may use at most 192 MiB of HBM per device.

v0:
```python
import jax
import jax.numpy as jnp
from jax import lax
from jax.sharding import PartitionSpec as P

HEAD_DIM = 128
EXPERTS = 32
FF = 768
BLOCK = 256
KB = 1024
MOST = 32


epsilon = 1e-06
rotary_base = 10000.0
masked_value = -1e30


def rms_scale(values, gain):
    inverse = lax.rsqrt(jnp.mean(values * values, axis=-1, keepdims=True) + epsilon)
    return values * inverse * gain


def rotate(values, positions, direction):
    halfway = values.shape[-1] // 2
    frequency = rotary_base ** (-jnp.arange(halfway).astype(jnp.float32) * 2.0 / values.shape[-1])
    angles = positions.astype(jnp.float32)[:, None] * frequency[None, :]
    cosine = jnp.cos(angles)[:, None, :]
    sine = direction * jnp.sin(angles)[:, None, :]
    leading = values[..., :halfway]
    trailing = values[..., halfway:]
    return jnp.concatenate(
        [leading * cosine - trailing * sine, trailing * cosine + leading * sine], axis=-1
    )


def gelu_product(gate_lin, up_lin):
    return jax.nn.gelu(gate_lin, approximate=True) * up_lin


def block_scores(queries, key_stack, offset, key_step, query_blocks, scaling):
    segment = lax.dynamic_slice_in_dim(key_stack, offset, key_step, 0)
    key_rows = segment[:, :, 0, :]
    value_token_rows = segment[:, :, 1, :]
    scores = (
        jnp.einsum("kgqd,nkd->kgqn", queries, key_rows, preferred_element_type=jnp.float32)
        * scaling
    )
    key_blocks = (offset + jnp.arange(key_step, dtype=jnp.int32)) // BLOCK
    allowed = key_blocks[None, :] <= query_blocks[:, None]
    scores = jnp.where(allowed[None, None], scores, masked_value)
    return (scores, key_rows, value_token_rows)


def shard_sum(query_g, key_g, value_g, output_g, router_g, gain_a, gain_b):
    return (
        lax.psum_scatter(query_g, "fsdp", scatter_dimension=0, tiled=True),
        lax.psum_scatter(key_g, "fsdp", scatter_dimension=0, tiled=True),
        lax.psum_scatter(value_g, "fsdp", scatter_dimension=0, tiled=True),
        lax.psum_scatter(output_g, "fsdp", scatter_dimension=0, tiled=True),
        lax.psum_scatter(router_g, "fsdp", scatter_dimension=0, tiled=True),
        lax.psum_scatter(gain_a, "fsdp", scatter_dimension=0, tiled=True),
        lax.psum_scatter(gain_b, "fsdp", scatter_dimension=0, tiled=True),
    )


def pair_sum(query_g, key_g, value_g, output_g, router_g, gain_a, gain_b, gate_g, up_g, down_g):
    return (
        lax.psum(query_g.astype(jnp.bfloat16), "sp").astype(jnp.float32),
        lax.psum(key_g.astype(jnp.bfloat16), "sp").astype(jnp.float32),
        lax.psum(value_g.astype(jnp.bfloat16), "sp").astype(jnp.float32),
        lax.psum(output_g.astype(jnp.bfloat16), "sp").astype(jnp.float32),
        lax.psum(router_g.astype(jnp.bfloat16), "sp").astype(jnp.float32),
        lax.psum(gain_a.astype(jnp.bfloat16), "sp").astype(jnp.float32),
        lax.psum(gain_b.astype(jnp.bfloat16), "sp").astype(jnp.float32),
        lax.psum(gate_g.astype(jnp.bfloat16), "sp").astype(jnp.float32),
        lax.psum(up_g.astype(jnp.bfloat16), "sp").astype(jnp.float32),
        lax.psum(down_g.astype(jnp.bfloat16), "sp").astype(jnp.float32),
    )


def body(
    tokens,
    cotangent,
    routes,
    attn_gain,
    query_weight,
    key_matrix,
    value_matrix,
    output_weight,
    moe_gain,
    router_weight,
    gate_weight,
    up_weight,
    down_weight,
):
    tok_rows = tokens.shape[0]
    model_width = tokens.shape[1]
    top_k = routes.shape[1]
    sp_count = lax.axis_size("sp")
    fsdp_count = lax.axis_size("fsdp")
    shard_index = lax.axis_index("fsdp")
    pair_index = lax.axis_index("sp")
    positions = (shard_index * sp_count + pair_index) * tok_rows + jnp.arange(
        tok_rows, dtype=jnp.int32
    )
    w_query, w_key, w_value, w_output, w_router, gain_attn, gain_moe = (
        lax.all_gather(query_weight, "fsdp", axis=0, tiled=True),
        lax.all_gather(key_matrix, "fsdp", axis=0, tiled=True),
        lax.all_gather(value_matrix, "fsdp", axis=0, tiled=True),
        lax.all_gather(output_weight, "fsdp", axis=0, tiled=True),
        lax.all_gather(router_weight, "fsdp", axis=0, tiled=True),
        lax.all_gather(attn_gain, "fsdp", axis=0, tiled=True),
        lax.all_gather(moe_gain, "fsdp", axis=0, tiled=True),
    )
    gain_one = gain_attn.astype(jnp.float32)
    gain_two = gain_moe.astype(jnp.float32)
    query_heads = w_query.shape[1] // HEAD_DIM
    kv_heads = w_key.shape[1] // HEAD_DIM
    query_group_count = query_heads // kv_heads
    local_kv = kv_heads // sp_count
    scaling = HEAD_DIM ** (-0.5)
    inputs = tokens.astype(jnp.float32)
    normalized_input = rms_scale(inputs, gain_one).astype(jnp.bfloat16)
    query_lin = jnp.dot(normalized_input, w_query, preferred_element_type=jnp.float32)
    key_linear = jnp.dot(normalized_input, w_key, preferred_element_type=jnp.float32)
    value_low = jnp.dot(normalized_input, w_value, preferred_element_type=jnp.float32).astype(
        jnp.bfloat16
    )
    query_rot = rotate(query_lin.reshape(tok_rows, query_heads, HEAD_DIM), positions, 1.0).astype(
        jnp.bfloat16
    )
    key_rot = rotate(key_linear.reshape(tok_rows, kv_heads, HEAD_DIM), positions, 1.0).astype(
        jnp.bfloat16
    )
    packed = jnp.stack([key_rot, value_low.reshape(tok_rows, kv_heads, HEAD_DIM)], axis=2).reshape(
        tok_rows, kv_heads * 2 * HEAD_DIM
    )
    query_seq, packed_seq = (
        lax.all_to_all(
            query_rot.reshape(tok_rows, query_heads * HEAD_DIM),
            "sp",
            split_axis=1,
            concat_axis=0,
            tiled=True,
        ),
        lax.all_to_all(packed, "sp", split_axis=1, concat_axis=0, tiled=True),
    )
    key_table = lax.all_gather(packed_seq, "fsdp", axis=0, tiled=True)
    query_rows = query_seq.shape[0]
    key_count = key_table.shape[0]
    key_stack = key_table.reshape(key_count, local_kv, 2, HEAD_DIM)
    queries = query_seq.reshape(query_rows, local_kv, query_group_count, HEAD_DIM).transpose(
        1, 2, 0, 3
    )
    query_offset = shard_index * query_rows
    query_blocks = (query_offset + jnp.arange(query_rows, dtype=jnp.int32)) // BLOCK
    key_step = min(KB, key_count)
    turn_count = (query_offset + query_rows - 1) // key_step + 1
    stat_shape = (local_kv, query_group_count, query_rows, 1)

    def max_step(block_index, carry):
        running_top, running_sum = carry
        scores, _, _ = block_scores(
            queries, key_stack, block_index * key_step, key_step, query_blocks, scaling
        )
        new_top = jnp.maximum(running_top, jnp.max(scores, axis=-1, keepdims=True))
        running_sum = running_sum * jnp.exp(running_top - new_top) + jnp.sum(
            jnp.exp(scores - new_top), axis=-1, keepdims=True
        )
        return (new_top, running_sum)

    running_top, running_sum = lax.fori_loop(
        0,
        turn_count,
        max_step,
        (jnp.full(stat_shape, masked_value, jnp.float32), jnp.zeros(stat_shape, jnp.float32)),
    )
    log_total = running_top + jnp.log(running_sum)

    def value_step(block_index, attended):
        scores, _, value_token_rows = block_scores(
            queries, key_stack, block_index * key_step, key_step, query_blocks, scaling
        )
        probs_low = jnp.exp(scores - log_total).astype(jnp.bfloat16)
        return attended + jnp.einsum(
            "kgqn,nkd->kgqd", probs_low, value_token_rows, preferred_element_type=jnp.float32
        )

    attended = lax.fori_loop(0, turn_count, value_step, jnp.zeros(queries.shape, jnp.float32))
    heads_low = (
        attended.astype(jnp.bfloat16)
        .transpose(2, 0, 1, 3)
        .reshape(query_rows, local_kv * query_group_count * HEAD_DIM)
    )
    heads_tok = lax.all_to_all(heads_low, "sp", split_axis=0, concat_axis=1, tiled=True)
    hidden = inputs + jnp.dot(heads_tok, w_output, preferred_element_type=jnp.float32)
    mixed = rms_scale(hidden, gain_two).astype(jnp.bfloat16)
    logits = jnp.dot(mixed, w_router, preferred_element_type=jnp.float32)
    expert_ids = jnp.arange(EXPERTS, dtype=jnp.int32)
    chosen = routes[:, :, None] == expert_ids[None, None, :]
    picked = jnp.sum(jnp.where(chosen, logits[:, None, :], 0.0), axis=-1)
    gates = jax.nn.softmax(picked, axis=-1)
    route_count = tok_rows * top_k
    flat_routes = routes.reshape(route_count)
    matches = (flat_routes[:, None] == expert_ids[None, :]).astype(jnp.int32)
    slot_rank = jnp.sum((jnp.cumsum(matches, axis=0) - matches) * matches, axis=1)
    columns = gate_weight.shape[1]
    local_count = max(1, columns // FF)
    owners = max(1, FF // columns)
    slot_count = local_count * MOST
    first_owner = flat_routes * FF // columns
    targets = []
    for owner in range(owners):
        target_dev = first_owner + owner
        local_expert = flat_routes - target_dev * columns // FF
        targets.append(target_dev * slot_count + local_expert * MOST + slot_rank)
    target_slots = jnp.stack(targets, axis=1).reshape(route_count * owners)
    sources = jnp.repeat(jnp.arange(route_count, dtype=jnp.int32), owners)
    slot_table = (
        jnp.full((fsdp_count * slot_count,), route_count, jnp.int32).at[target_slots].set(sources)
    )
    padded_mixed = jnp.concatenate([mixed, jnp.zeros((1, model_width), jnp.bfloat16)], axis=0)
    outgoing = jnp.take(padded_mixed, slot_table // top_k, axis=0)
    inbound = lax.all_to_all(outgoing, "fsdp", split_axis=0, concat_axis=0, tiled=True).reshape(
        fsdp_count, local_count, MOST, model_width
    )
    gate_cols = gate_weight.reshape(model_width, local_count, columns // local_count)
    up_cols = up_weight.reshape(model_width, local_count, columns // local_count)
    down_rows = down_weight.reshape(local_count, columns // local_count, model_width)
    gate_lin = jnp.einsum("sgmd,dgc->sgmc", inbound, gate_cols, preferred_element_type=jnp.float32)
    up_lin = jnp.einsum("sgmd,dgc->sgmc", inbound, up_cols, preferred_element_type=jnp.float32)
    inner_act = gelu_product(gate_lin, up_lin).astype(jnp.bfloat16)
    partial_out = jnp.einsum(
        "sgmc,gcd->sgmd", inner_act, down_rows, preferred_element_type=jnp.float32
    )
    returned = lax.all_to_all(
        partial_out.reshape(fsdp_count * slot_count, model_width).astype(jnp.bfloat16),
        "fsdp",
        split_axis=0,
        concat_axis=0,
        tiled=True,
    ).astype(jnp.float32)
    expert_out = (
        jnp.take(returned, target_slots, axis=0)
        .reshape(tok_rows, top_k, owners, model_width)
        .sum(axis=2)
    )
    mixture = jnp.sum(gates[:, :, None] * expert_out, axis=1)
    output = (hidden + mixture).astype(jnp.bfloat16)
    out_grad = cotangent.astype(jnp.float32)
    gate_grad_k = jnp.sum(expert_out * out_grad[:, None, :], axis=-1)
    route_grad = (
        (gates[:, :, None] * out_grad[:, None, :])
        .astype(jnp.bfloat16)
        .reshape(route_count, model_width)
    )
    padded_grad = jnp.concatenate([route_grad, jnp.zeros((1, model_width), jnp.bfloat16)], axis=0)
    grad_in = lax.all_to_all(
        jnp.take(padded_grad, slot_table, axis=0), "fsdp", split_axis=0, concat_axis=0, tiled=True
    ).reshape(fsdp_count, local_count, MOST, model_width)
    inner_grad = jnp.einsum(
        "sgmd,gcd->sgmc", grad_in, down_rows, preferred_element_type=jnp.float32
    )
    down_grad = jnp.einsum(
        "sgmc,sgmd->gcd", inner_act, grad_in, preferred_element_type=jnp.float32
    ).reshape(columns, model_width)
    _, product_back = jax.vjp(gelu_product, gate_lin, up_lin)
    gate_lin_grad, up_lin_grad = product_back(inner_grad)
    gate_low = gate_lin_grad.astype(jnp.bfloat16)
    up_low = up_lin_grad.astype(jnp.bfloat16)
    gate_grad = jnp.einsum(
        "sgmd,sgmc->dgc", inbound, gate_low, preferred_element_type=jnp.float32
    ).reshape(model_width, columns)
    up_grad = jnp.einsum(
        "sgmd,sgmc->dgc", inbound, up_low, preferred_element_type=jnp.float32
    ).reshape(model_width, columns)
    mixed_part = jnp.einsum(
        "sgmc,dgc->sgmd", gate_low, gate_cols, preferred_element_type=jnp.float32
    )
    mixed_part = mixed_part + jnp.einsum(
        "sgmc,dgc->sgmd", up_low, up_cols, preferred_element_type=jnp.float32
    )
    mixed_back = lax.all_to_all(
        mixed_part.reshape(fsdp_count * slot_count, model_width).astype(jnp.bfloat16),
        "fsdp",
        split_axis=0,
        concat_axis=0,
        tiled=True,
    ).astype(jnp.float32)
    mixed_grad = (
        jnp.take(mixed_back, target_slots, axis=0)
        .reshape(tok_rows, top_k * owners, model_width)
        .sum(axis=1)
    )
    picked_grad = gates * (gate_grad_k - jnp.sum(gates * gate_grad_k, axis=-1, keepdims=True))
    logit_grad = jnp.sum(jnp.where(chosen, picked_grad[:, :, None], 0.0), axis=1).astype(
        jnp.bfloat16
    )
    router_grad = jnp.dot(mixed.T, logit_grad, preferred_element_type=jnp.float32)
    mixed_grad = mixed_grad + jnp.dot(logit_grad, w_router.T, preferred_element_type=jnp.float32)
    _, second_back = jax.vjp(rms_scale, hidden, gain_two)
    hidden_norm_grad, moe_gain_grad = second_back(mixed_grad)
    hidden_grad = out_grad + hidden_norm_grad
    attn_grad = hidden_grad.astype(jnp.bfloat16)
    output_grad = jnp.dot(heads_tok.T, attn_grad, preferred_element_type=jnp.float32)
    heads_grad = jnp.dot(attn_grad, w_output.T, preferred_element_type=jnp.float32).astype(
        jnp.bfloat16
    )
    heads_grad_seq = lax.all_to_all(heads_grad, "sp", split_axis=1, concat_axis=0, tiled=True)
    head_grads = heads_grad_seq.reshape(
        query_rows, local_kv, query_group_count, HEAD_DIM
    ).transpose(1, 2, 0, 3)
    delta_row = jnp.sum(head_grads.astype(jnp.float32) * attended, axis=-1, keepdims=True)

    def grad_step(block_index, carry):
        query_acc, key_acc = carry
        offset = block_index * key_step
        scores, key_rows, value_token_rows = block_scores(
            queries, key_stack, offset, key_step, query_blocks, scaling
        )
        probs = jnp.exp(scores - log_total)
        probs_low = probs.astype(jnp.bfloat16)
        prob_grad = jnp.einsum(
            "kgqd,nkd->kgqn", head_grads, value_token_rows, preferred_element_type=jnp.float32
        )
        score_low = (probs * (prob_grad - delta_row)).astype(jnp.bfloat16)
        query_acc = query_acc + jnp.einsum(
            "kgqn,nkd->kgqd", score_low, key_rows, preferred_element_type=jnp.float32
        )
        key_part = (
            jnp.einsum("kgqn,kgqd->nkd", score_low, queries, preferred_element_type=jnp.float32)
            * scaling
        )
        value_part = jnp.einsum(
            "kgqn,kgqd->nkd", probs_low, head_grads, preferred_element_type=jnp.float32
        )
        current = lax.dynamic_slice_in_dim(key_acc, offset, key_step, 0)
        key_acc = lax.dynamic_update_slice_in_dim(
            key_acc, current + jnp.stack([key_part, value_part], axis=2), offset, 0
        )
        return (query_acc, key_acc)

    query_acc, key_acc = lax.fori_loop(
        0,
        turn_count,
        grad_step,
        (
            jnp.zeros(queries.shape, jnp.float32),
            jnp.zeros((key_count, local_kv, 2, HEAD_DIM), jnp.float32),
        ),
    )
    kv_grad = lax.psum_scatter(
        key_acc.reshape(key_count, local_kv * 2 * HEAD_DIM), "fsdp", scatter_dimension=0, tiled=True
    ).astype(jnp.bfloat16)
    query_grad_low = (
        (query_acc * scaling)
        .astype(jnp.bfloat16)
        .transpose(2, 0, 1, 3)
        .reshape(query_rows, local_kv * query_group_count * HEAD_DIM)
    )
    query_grad_tok, kv_grad_tok = (
        lax.all_to_all(query_grad_low, "sp", split_axis=0, concat_axis=1, tiled=True),
        lax.all_to_all(kv_grad, "sp", split_axis=0, concat_axis=1, tiled=True),
    )
    kv_parts = kv_grad_tok.reshape(tok_rows, kv_heads, 2, HEAD_DIM)
    query_lin_grad = (
        rotate(
            query_grad_tok.reshape(tok_rows, query_heads, HEAD_DIM).astype(jnp.float32),
            positions,
            -1.0,
        )
        .astype(jnp.bfloat16)
        .reshape(tok_rows, query_heads * HEAD_DIM)
    )
    key_lin_grad = (
        rotate(kv_parts[:, :, 0, :].astype(jnp.float32), positions, -1.0)
        .astype(jnp.bfloat16)
        .reshape(tok_rows, kv_heads * HEAD_DIM)
    )
    value_grad_low = kv_parts[:, :, 1, :].reshape(tok_rows, kv_heads * HEAD_DIM)
    query_grad = jnp.dot(normalized_input.T, query_lin_grad, preferred_element_type=jnp.float32)
    key_grad = jnp.dot(normalized_input.T, key_lin_grad, preferred_element_type=jnp.float32)
    value_grad = jnp.dot(normalized_input.T, value_grad_low, preferred_element_type=jnp.float32)
    normed_grad = jnp.dot(query_lin_grad, w_query.T, preferred_element_type=jnp.float32)
    normed_grad = normed_grad + jnp.dot(key_lin_grad, w_key.T, preferred_element_type=jnp.float32)
    normed_grad = normed_grad + jnp.dot(
        value_grad_low, w_value.T, preferred_element_type=jnp.float32
    )
    _, first_back = jax.vjp(rms_scale, inputs, gain_one)
    input_norm_grad, attn_gain_grad = first_back(normed_grad)
    input_grad = (hidden_grad + input_norm_grad).astype(jnp.bfloat16)
    whole = pair_sum(
        query_grad,
        key_grad,
        value_grad,
        output_grad,
        router_grad,
        attn_gain_grad,
        moe_gain_grad,
        gate_grad,
        up_grad,
        down_grad,
    )
    shards = shard_sum(whole[0], whole[1], whole[2], whole[3], whole[4], whole[5], whole[6])
    summed = tuple(shards) + tuple(whole[7:])
    return (
        output,
        input_grad,
        summed[0],
        summed[1],
        summed[2],
        summed[3],
        summed[4],
        summed[7],
        summed[8],
        summed[9],
        summed[5],
        summed[6],
    )


def solution(mesh):
    in_specs = (
        P(("fsdp", "sp"), None),
        P(("fsdp", "sp"), None),
        P(("fsdp", "sp"), None),
        P("fsdp"),
        P("fsdp", None),
        P("fsdp", None),
        P("fsdp", None),
        P("fsdp", None),
        P("fsdp"),
        P("fsdp", None),
        P(None, "fsdp"),
        P(None, "fsdp"),
        P("fsdp", None),
    )
    out_specs = (
        P(("fsdp", "sp"), None),
        P(("fsdp", "sp"), None),
        P("fsdp", None),
        P("fsdp", None),
        P("fsdp", None),
        P("fsdp", None),
        P("fsdp", None),
        P(None, "fsdp"),
        P(None, "fsdp"),
        P("fsdp", None),
        P("fsdp"),
        P("fsdp"),
    )
    return jax.shard_map(body, mesh=mesh, in_specs=in_specs, out_specs=out_specs, check_vma=False)
```

profile of v0, /device:TPU:0, one launch (start us, length us, event | category | flops | bytes accessed | tf_op | source)
XLA Modules:
  0.0 1800.9 jit_solution(16716291259668577717)
XLA Ops:
  11.7 36.0 %all-reduce.7 = (bf16[1536]{0:T(1024)(128)(2,1)S(1)}, bf16[1536]{0:T(1024)(128)(2,1)S(1)}) all-reduce(bf16[1536]{0:T(1024)(128)(2,1)S(1)} %dynamic-update-slice, bf16[1536]{0:T(1024)(128)(2,1)S(1)} %dynamic-update-slice.1), channel_id=1, replica_groups=mesh['fsdp'=16,'sp'=2] {'fsdp'}, use_global_device_ids=true, to_apply=%add.2 | all-reduce | flops 3072 | bytes 12288
  49.0 22.9 %all_gather.26 = bf16[1536,256]{1,0:T(8,128)(2,1)S(1)} all-gather(bf16[96,256]{1,0:T(8,128)(2,1)} %param.27), channel_id=1, replica_groups=mesh['fsdp'=16,'sp'=2] {'fsdp'}, dimensions={0}, use_global_device_ids=true | all-gather | bytes 835584 | tf_op jit(solution)/shard_map/all_gather | solution.py:110
  75.1 21.0 %all_gather.25 = bf16[1536,256]{1,0:T(8,128)(2,1)S(1)} all-gather(bf16[96,256]{1,0:T(8,128)(2,1)S(1)} %copy-done.28), channel_id=1, replica_groups=mesh['fsdp'=16,'sp'=2] {'fsdp'}, dimensions={0}, use_global_device_ids=true | all-gather | bytes 835584 | tf_op jit(solution)/shard_map/all_gather | solution.py:109
  97.5 7.0 all_to_all.120
  110.6 4.3 fusion.127
  115.8 3.5 all-to-all-start.1
  119.9 23.2 %all-gather.5.cloned.1.call-done = bf16[4096,256]{1,0:T(8,128)(2,1)} async-done(((bf16[256,256]{1,0:T(8,128)(2,1)}), bf16[4096,256]{1,0:T(8,128)(2,1)}) %all-gather.5.cloned.1.call-update) | async-done | bytes 2097168 | tf_op jit(solution)/shard_map/all_gather | solution.py:149
  149.4 3.7 while.43
  153.2 4.0 while.44
  153.7 3.5 fusion.188
  158.4 3.5 all-to-all-start.2
  162.5 35.1 %all-gather.9.cloned.1.call-done = bf16[1536,1536]{1,0:T(8,128)(2,1)} async-done(((bf16[96,1536]{1,0:T(8,128)(2,1)}), bf16[1536,1536]{1,0:T(8,128)(2,1)}) %all-gather.9.cloned.1.call-update) | async-done | bytes 4718608 | tf_op jit(solution)/shard_map/all_gather | solution.py:111
  197.6 3.4 multiply_reduce_fusion.5
  202.8 5.6 gather_fusion
  208.4 3.9 broadcast_select_fusion.1
  212.3 3.7 all-to-all-start.3
  216.1 10.6 reshape.824
  226.7 10.6 reshape.825
  237.3 38.0 %all-to-all-done.3 = bf16[16,64,1536]{2,1,0:T(8,128)(2,1)S(1)} async-done(((bf16[16,64,1536]{2,1,0:T(8,128)(2,1)}), bf16[16,64,1536]{2,1,0:T(8,128)(2,1)S(1)}, u32[]{:S(2)}, u32[]{:S(2)}) %all-to-all-start.3) | async-done | bytes 3145760 | tf_op jit(solution)/shard_map/all_to_all | solution.py:225
  275.4 6.1 fusion.67
  281.5 4.4 fusion.81
  290.7 15.6 all-to-all-start.4
  311.6 62.7 %all-gather = bf16[16,96,32]{1,2,0:T(8,128)(2,1)S(1)} all-gather(bf16[1,96,32]{1,2,0:T(8,128)(2,1)} %bitcast.430), channel_id=1, replica_groups=mesh['fsdp'=16,'sp'=2] {'fsdp'}, dimensions={0}, use_global_device_ids=true | all-gather | bytes 104448 | tf_op jit(solution)/shard_map/all_gather | solution.py:112
  382.3 5.5 bitcast_convert_fusion.4
  387.8 7.3 gather_fusion.2
  395.2 3.9 multiply_reduce_fusion
  406.5 5.6 gather_fusion.1
  414.5 86.6 %all_to_all.121 = bf16[16,64,1536]{2,1,0:T(8,128)(2,1)S(1)} all-to-all(bf16[16,64,1536]{2,1,0:T(8,128)(2,1)S(1)} %broadcast_select_fusion), channel_id=1, replica_groups=mesh['fsdp'=16,'sp'=2] {'fsdp'}, dimensions={0} | all-to-all | bytes 6291456 | tf_op jit(solution)/shard_map/all_to_all | solution.py:259
  501.2 8.5 fusion.80
  517.4 5.6 all-to-all-start.6
  528.6 3.9 multiply_reduce_fusion.1
  532.5 49.8 %all-to-all-done.6 = bf16[16,64,1536]{2,1,0:T(8,128)(2,1)} async-done(((bf16[16,64,1536]{2,1,0:T(8,128)(2,1)}), bf16[16,64,1536]{2,1,0:T(8,128)(2,1)}, u32[]{:S(2)}, u32[]{:S(2)}) %all-to-all-start.6) | async-done | bytes 3145760 | tf_op jit(solution)/shard_map/all_to_all | solution.py:284
  582.3 5.5 bitcast_convert_fusion.3
  587.8 6.6 gather_fusion.3
  609.6 4.0 convolution_convert_fusion.5
  614.6 3.5 all-to-all-start.7
  618.9 6.9 all-to-all-done.7
  630.1 20.9 %while.45 = (s32[]{:T(128)}, f32[1,6,256,128]{3,2,1,0:T(8,128)S(1)}, f32[4096,1,2,128]{0,3,2,1:T(8,128)}, s32[]{:T(128)}, bf16[4096,1,2,128]{3,0,2,1:T(8,128)(2,...) while((s32[]{:T(128)}, ...), condition=%wide.region_23.25_spmd.clone, body=%wide.region_22.24_spmd.clone.sunk | while | flops 2030129152 | bytes 70807840 | solution.py:344
  630.3 4.6 fusion.196
  635.2 4.9 fusion.197
  644.1 4.4 fusion.199
  652.4 6.2 bitcast_convert_fusion.2
  658.6 6.7 copy.174
  665.3 6.2 bitcast_convert_fusion.1
  671.5 6.7 copy.176
  678.2 6.2 bitcast_convert_fusion
  685.6 3.7 all-to-all-start.8
  689.4 3.6 convolution_convert_fusion
  696.4 98.5 %reduce-scatter.9.cloned.1.call-done = f32[256,256]{0,1:T(8,128)} async-done(((f32[4096,256]{0,1:T(8,128)}), f32[256,256]{0,1:T(8,128)}) %reduce-scatter.9.cloned.1.call-update) | async-done | bytes 262160 | tf_op jit(solution)/shard_map/reduce_scatter | solution.py:353
  796.5 3.4 all-to-all-start.9
  800.0 3.7 convolution_convert_fusion.1
  807.3 567.5 %all-reduce.12.cloned.1.call-done = (bf16[1536,1536]{1,0:T(8,128)(2,1)}, bf16[1536,256]{1,0:T(8,128)(2,1)}, bf16[1536,256]{1,0:T(8,128)(2,1)}, bf16[1536,1536]{1...) async-done(((bf16[1536,1536]{1,0:T(8,128)(2,1)}, ...) | async-done | bytes 25264144 | tf_op jit(solution)/shard_map/psum | solution.py:69
  1380.7 7.3 convert_element_type.298
  1388.1 7.4 convert_element_type.304
  1396.3 4.1 fusion.136
  1401.4 5.0 all-reduce.8
  1406.4 60.7 %all-reduce.6 = (f32[1536]{0:T(1024)S(1)}, f32[1536]{0:T(1024)S(1)}) all-reduce(bf16[1536]{0:T(1024)(128)(2,1)S(1)} %get-tuple-element.523, bf16[1536]{0:T(1024)(128)(2,1)S(1)} %get-tuple-element.524), channel_id=8, replica_groups=mesh['fsdp'=16,'sp'=2] {'fsdp'}, use_global_device_ids=true, to_apply=%region_41.43.clone | all-reduce | flops 3072 | bytes 18432
  1469.3 7.8 convert_element_type.310
  1477.2 5.1 convert_element_type.314
  1482.2 5.1 convert_element_type.317
  1488.8 10.9 reduce-scatter.13.cloned.1.call-done
  1499.6 62.7 %reduce-scatter.15.cloned.1.call-done = f32[96,256]{1,0:T(8,128)} async-done(((f32[1536,256]{1,0:T(8,128)}), f32[96,256]{1,0:T(8,128)}) %reduce-scatter.15.cloned.1.call-update) | async-done | bytes 98320 | tf_op jit(solution)/shard_map/reduce_scatter | solution.py:59
  1562.4 115.6 %reduce-scatter.11.cloned.1.call-done = f32[96,1536]{1,0:T(8,128)} async-done(((f32[1536,1536]{1,0:T(8,128)}), f32[96,1536]{1,0:T(8,128)}) %reduce-scatter.11.cloned.1.call-update) | async-done | bytes 589840 | tf_op jit(solution)/shard_map/reduce_scatter | solution.py:57
  1678.0 115.7 %reduce-scatter.17.cloned.1.call-done = f32[96,1536]{1,0:T(8,128)} async-done(((f32[1536,1536]{1,0:T(8,128)}), f32[96,1536]{1,0:T(8,128)}) %reduce-scatter.17.cloned.1.call-update) | async-done | bytes 589840 | tf_op jit(solution)/shard_map/reduce_scatter | solution.py:60
  (292 shorter events, 121.7 us)
Async XLA Ops:
  7.2 89.8 %copy-start.2 = (bf16[128,1536]{1,0:T(8,128)(2,1)S(1)}, bf16[128,1536]{1,0:T(8,128)(2,1)}, u32[]{:S(2)}) copy-start(bf16[128,1536]{1,0:T(8,128)(2,1)} %param.21) | copy-start | bytes 1179652
  7.2 67.9 %copy-start.28 = (bf16[96,256]{1,0:T(8,128)(2,1)S(1)}, bf16[96,256]{1,0:T(8,128)(2,1)}, u32[]{:S(2)}) copy-start(bf16[96,256]{1,0:T(8,128)(2,1)} %param.26) | copy-start | bytes 147460
  7.2 103.3 %all-gather.7.cloned.1.call-start = ((), (), s32[]{:S(2)}) async-start(), calls=%async_computation.17 | async-start | bytes 5013504 | tf_op jit(solution)/shard_map/all_gather | solution.py:108
  7.9 135.2 %all-gather.5.cloned.1.call-start = ((), (), s32[]{:S(2)}) async-start(), calls=%async_computation.16 | async-start | bytes 2228224 | tf_op jit(solution)/shard_map/all_gather | solution.py:149
  47.8 62.8 %copy-start.24 = (f32[1536]{0:T(1024)}, f32[1536]{0:T(1024)S(1)}, u32[]{:S(2)}) copy-start(f32[1536]{0:T(1024)S(1)} %convert_element_type.256) | copy-start | bytes 18436
  49.0 57.3 %copy-start.40 = (f32[128]{0:T(128)}, f32[128]{0:T(128)S(1)}, u32[]{:S(2)}) copy-start(f32[128]{0:T(128)S(1)} %fusion.98) | copy-start | bytes 1540
  49.0 57.0 %copy-start.31 = (s32[128,4]{0,1:T(4,128)S(1)}, s32[128,4]{0,1:T(4,128)}, u32[]{:S(2)}) copy-start(s32[128,4]{0,1:T(4,128)} %param.23) | copy-start | bytes 6148
  49.0 61.6 %copy-start.29 = (f32[128]{0:T(128)}, f32[128]{0:T(128)S(1)}, u32[]{:S(2)}) copy-start(f32[128]{0:T(128)S(1)} %fusion.122) | copy-start | bytes 1540
  75.1 39.8 %copy-start.22 = (f32[128,64]{0,1:T(8,128)}, f32[128,64]{0,1:T(8,128)S(1)}, u32[]{:S(2)}) copy-start(f32[128,64]{0,1:T(8,128)S(1)} %get-tuple-element.561) | copy-start | bytes 98308
  105.2 92.3 %all-gather.9.cloned.1.call-start = ((), (), s32[]{:S(2)}) async-start(), calls=%async_computation.18 | async-start | bytes 5013504 | tf_op jit(solution)/shard_map/all_gather | solution.py:111
  115.8 32.7 %all-to-all-start.1 = ((bf16[128,2,768]{0,2,1:T(8,128)(2,1)}), bf16[128,2,768]{0,2,1:T(8,128)(2,1)S(1)}, u32[]{:S(2)}, u32[]{:S(2)}) async-start(bf16[128,2,768]{0,2,1:T(8,128)(2,1)} %bitcast.10), calls=%async_computation.1 | async-start | bytes 786432 | tf_op jit(solution)/shard_map/all_to_all | solution.py:140
  157.2 43.7 %copy-start.7 = (f32[1,6,256,128]{3,2,1,0:T(8,128)}, f32[1,6,256,128]{3,2,1,0:T(8,128)S(1)}, u32[]{:S(2)}) copy-start(f32[1,6,256,128]{3,2,1,0:T(8,128)S(1)} %get-tuple-element.332) | copy-start | bytes 2359300
  157.2 43.7 %copy-start.37 = (f32[1,6,256,1]{2,1,3,0:T(8,128)}, f32[1,6,256,1]{2,1,3,0:T(8,128)S(1)}, u32[]{:S(2)}) copy-start(f32[1,6,256,1]{2,1,3,0:T(8,128)S(1)} %get-tuple-element.912) | copy-start | bytes 18436
  158.4 39.2 %all-to-all-start.2 = ((bf16[2,128,768]{1,2,0:T(8,128)(2,1)}), bf16[2,128,768]{1,2,0:T(8,128)(2,1)S(1)}, u32[]{:S(2)}, u32[]{:S(2)}) async-start(bf16[2,128,768]{1,2,0:T(8,128)(2,1)} %copy.143), calls=%async_computation.2 | async-start | bytes 786432 | tf_op jit(solution)/shard_map/all_to_all | solution.py:196
  197.6 3.4 copy-start.13
  201.0 7.4 copy-start.39
  212.3 63.0 %all-to-all-start.3 = ((bf16[16,64,1536]{2,1,0:T(8,128)(2,1)}), bf16[16,64,1536]{2,1,0:T(8,128)(2,1)S(1)}, u32[]{:S(2)}, u32[]{:S(2)}) async-start(bf16[16,64,1536]{2,1,0:T(8,128)(2,1)} %broadcast_select_fusion.1), calls=%async_computation.3 | async-start | bytes 6291456 | tf_op jit(solution)/shard_map/all_to_all | solution.py:225
  275.4 6.1 copy-start.16
  275.4 6.2 copy-start.15
  275.4 10.5 slice-start.8
  281.5 4.4 copy-start.47
  281.5 4.4 slice-start.9
  290.7 15.6 copy-start.21
  290.7 91.6 %all-to-all-start.4 = ((bf16[16,64,1536]{2,1,0:T(8,128)(2,1)}), bf16[16,64,1536]{2,1,0:T(8,128)(2,1)}, u32[]{:S(2)}, u32[]{:S(2)}) async-start(bf16[16,64,1536]{2,1,0:T(8,128)(2,1)} %bitcast.30), calls=%async_computation.4 | async-start | bytes 6291456 | tf_op jit(solution)/shard_map/all_to_all | solution.py:237
  378.6 9.2 copy-start.34
  406.5 5.6 copy-start.36
  412.1 89.0 %copy-start.48 = (f32[2,16,32,768]{3,2,1,0:T(8,128)S(1)}, f32[2,16,32,768]{3,2,1,0:T(8,128)}, u32[]{:S(2)}) copy-start(f32[2,16,32,768]{3,2,1,0:T(8,128)} %copy-done.47) | copy-start | bytes 9437188
  414.5 95.2 %slice-start.6 = ((s8[4718592]{0:T(1024)(128)(4,1)}), s8[4194304]{0:T(1024)(128)(4,1)S(1)}, s32[]{:S(2)}) async-start(s8[4718592]{0:T(1024)(128)(4,1)} %bitcast.396), calls=%async_computation.32 | async-start | bytes 8388608
  414.5 97.9 %slice-start.4 = ((s8[4718592]{0:T(1024)(128)(4,1)}), s8[4194304]{0:T(1024)(128)(4,1)S(1)}, s32[]{:S(2)}) async-start(s8[4718592]{0:T(1024)(128)(4,1)} %bitcast.392), calls=%async_computation.30 | async-start | bytes 8388608
  501.1 8.5 copy-start.17
  501.1 8.6 slice-start.7
  501.1 11.3 slice-start.5
  517.4 5.6 copy-start.8
  517.4 65.0 %all-to-all-start.6 = ((bf16[16,64,1536]{2,1,0:T(8,128)(2,1)}), bf16[16,64,1536]{2,1,0:T(8,128)(2,1)}, u32[]{:S(2)}, u32[]{:S(2)}) async-start(bf16[16,64,1536]{2,1,0:T(8,128)(2,1)} %bitcast.40), calls=%async_computation.6 | async-start | bytes 6291456 | tf_op jit(solution)/shard_map/all_to_all | solution.py:284
  609.6 8.5 copy-start.12
  613.6 13.8 copy-start.18
  614.6 11.2 all-to-all-start.7
  618.0 176.9 %reduce-scatter.9.cloned.1.call-start = ((), (), s32[]{:S(2)}) async-start(), calls=%async_computation.19 | async-start | bytes 4456448 | tf_op jit(solution)/shard_map/reduce_scatter | solution.py:353
  644.0 4.5 copy-start.1
  658.6 6.7 copy-start.44
  671.5 6.8 copy-start.50
  684.4 4.9 copy-start.6
  684.4 4.9 copy-start.14
  685.6 10.6 all-to-all-start.8
  689.3 6.9 copy-start.23
  689.3 6.9 copy-start.27
  692.9 107.1 %copy-start.3 = (bf16[128,1536]{1,0:T(8,128)(2,1)S(1)}, bf16[128,1536]{1,0:T(8,128)(2,1)}, u32[]{:S(2)}) copy-start(bf16[128,1536]{1,0:T(8,128)(2,1)} %param.21) | copy-start | bytes 1179652
  692.9 107.1 %copy-start.25 = (f32[1536]{0:T(1024)S(1)}, f32[1536]{0:T(1024)}, u32[]{:S(2)}) copy-start(f32[1536]{0:T(1024)} %copy-done.24) | copy-start | bytes 18436
  692.9 107.1 %copy-start.30 = (f32[128]{0:T(128)S(1)}, f32[128]{0:T(128)}, u32[]{:S(2)}) copy-start(f32[128]{0:T(128)} %copy-done.29) | copy-start | bytes 1540
  796.5 7.8 all-to-all-start.9
  799.9 574.8 %all-reduce.12.cloned.1.call-start = ((), (), s32[]{:S(2)}) async-start(), calls=%async_computation.25 | async-start | bytes 50528256 | tf_op jit(solution)/shard_map/psum | solution.py:69
  807.2 680.1 %reduce-scatter.19.cloned.1.call-start = ((), (), s32[]{:S(2)}) async-start(), calls=%async_computation.24 | async-start | bytes 835584
  1374.8 4.6 copy-start.26
  1376.8 122.8 %reduce-scatter.13.cloned.1.call-start = ((), (), s32[]{:S(2)}) async-start(), calls=%async_computation.21 | async-start | bytes 1671168 | tf_op jit(solution)/shard_map/reduce_scatter | solution.py:58
  1379.3 183.0 %reduce-scatter.15.cloned.1.call-start = ((), (), s32[]{:S(2)}) async-start(), calls=%async_computation.22 | async-start | bytes 1671168 | tf_op jit(solution)/shard_map/reduce_scatter | solution.py:59
  1380.7 297.3 %reduce-scatter.11.cloned.1.call-start = ((), (), s32[]{:S(2)}) async-start(), calls=%async_computation.20 | async-start | bytes 10027008 | tf_op jit(solution)/shard_map/reduce_scatter | solution.py:57
  1388.1 405.6 %reduce-scatter.17.cloned.1.call-start = ((), (), s32[]{:S(2)}) async-start(), calls=%async_computation.23 | async-start | bytes 10027008 | tf_op jit(solution)/shard_map/reduce_scatter | solution.py:60
  1395.5 4.9 copy-start.10
  1396.3 4.6 copy-start.20
  1400.5 67.9 %copy-start.41 = (f32[128]{0:T(128)S(1)}, f32[128]{0:T(128)}, u32[]{:S(2)}) copy-start(f32[128]{0:T(128)} %copy-done.40) | copy-start | bytes 1540
  1468.3 8.8 slice-start.2
  1469.3 7.8 slice-start.3
  1469.3 12.9 slice-start
  1477.2 5.1 slice-start.1
  (15 other events, 25.1 us)
Sparse Core Ops, SparseCore 0:
  10.3 61.5 all-gather.6
  105.4 37.6 all-gather.4
  145.4 52.1 all-gather.8
  651.2 143.7 reduce-scatter.8
  807.4 567.3 all-reduce.11
  1378.2 58.2 reduce-scatter.18
  1441.1 58.4 reduce-scatter.12
  1503.9 58.4 reduce-scatter.14
  1567.6 110.3 reduce-scatter.10
  1682.5 111.0 reduce-scatter.16
where the time goes:
time: 1810 us; the launch traced here: 1800 us
  waiting for transfers between devices  1130 us (62%)
  blocking collectives  302 us (17%)
  local copies, waits for them, and re-layouts  119 us (7%)
  matrix products  102 us (6%)
  other arithmetic  88 us (5%)
  starting transfers between devices  42.8 us (2%)
    psum x1, waiting for transfers between devices, pair_sum(): lax.psum(query_g.astype(jnp.bfloat16), 'sp').astype(jnp.float32)  567 us
    reduce_scatter x1, waiting for transfers between devices, shard_sum(): lax.psum_scatter(output_g, 'fsdp', scatter_dimension=0, tiled=True)  116 us
    reduce_scatter x1, waiting for transfers between devices, shard_sum(): lax.psum_scatter(query_g, 'fsdp', scatter_dimension=0, tiled=True)  116 us
    reduce_scatter x1, waiting for transfers between devices, body(): lax.psum_scatter(key_acc.reshape(key_count, local_kv * 2 * HEAD_DIM), 'fs...  98.5 us
    unnamed x2, blocking collectives  96.7 us
    all_to_all x1, blocking collectives, body(): lax.all_to_all(jnp.take(padded_grad, slot_table, axis=0), 'fsdp', split_a...  86.6 us
    reduce_scatter x1, waiting for transfers between devices, shard_sum(): lax.psum_scatter(value_g, 'fsdp', scatter_dimension=0, tiled=True)  62.7 us
    all_gather x1, blocking collectives, body(): lax.all_gather(router_weight, 'fsdp', axis=0, tiled=True)  62.7 us
  transfers between devices with their start and end apart: 18, of which 13 were waited for; matrix products, arithmetic and copies ran while one was open for 9% of the time, Pallas kernels for 0%

commit v1 on v0

v1 whole, which is shorter than its diff:
```python
import functools

import jax
import jax.numpy as jnp
from jax import lax
from jax.experimental import pallas as pl
from jax.experimental.pallas import tpu as pltpu
from jax.sharding import PartitionSpec as P

HEAD_DIM = 128
EXPERTS = 32
FF = 768
BLOCK = 256
MOST = 32
CORES = 2
RING = 4

epsilon = 1e-06
rotary_base = 10000.0
masked_value = -1e30
log2e = 1.4426950408889634

bf16 = jnp.bfloat16
f32 = jnp.float32


def dot(a, b):
    return jnp.dot(a, b, preferred_element_type=f32)


def dot_tn(a, b):
    return lax.dot_general(a, b, (((0,), (0,)), ((), ())), preferred_element_type=f32)


def dot_nt(a, b):
    return lax.dot_general(a, b, (((1,), (1,)), ((), ())), preferred_element_type=f32)


class Plane:
    def __init__(self, count):
        self.count = count
        self.rows = count // (RING * CORES)
        self.names = [
            (k, j, m) for k in range(RING) for j in range(self.rows) for m in range(CORES)
        ]

    def index(self, z, y, c):
        return (z * self.rows + y) * CORES + c

    def place(self, i):
        return i // (self.rows * CORES), (i // CORES) % self.rows, i % CORES

    def sources(self, me):
        z, y, c = self.place(me)
        return jnp.stack(
            [
                self.index((z + RING - k) % RING, (y + self.rows - j) % self.rows, (c + m) % CORES)
                for k, j, m in self.names
            ]
        ).astype(jnp.int32)

    def positions(self, me):
        z, y, c = self.place(me)
        got = []
        for g in range(self.count):
            gz, gy, gc = self.place(g)
            got.append(
                self.index((z + RING - gz) % RING, (y + self.rows - gy) % self.rows, (c + gc) % CORES)
            )
        return jnp.stack(got).astype(jnp.int32)

    def along(self, which):
        pairs = []
        for i in range(self.count):
            at = list(self.place(i))
            size = (RING, self.rows, CORES)[which]
            at[which] = (at[which] + 1) % size
            pairs.append((i, self.index(*at)))
        return pairs

    def shift(self, value, which):
        return lax.ppermute(value, "fsdp", self.along(which))

    def gather(self, block):
        got = {}
        ring = block
        for k in range(RING):
            if k:
                ring = self.shift(ring, 0)
            row = ring
            for j in range(self.rows):
                if j:
                    row = self.shift(row, 1)
                got[k, j, 0] = row
                got[k, j, 1] = self.shift(row, 2)
        return [got[name] for name in self.names]

    def scatter(self, parts, group=True):
        held = []
        for k in range(RING):
            other = self.shift(parts[k][1].astype(bf16), 2)
            both = [parts[k][0][j].astype(f32) + other[j].astype(f32) for j in range(self.rows)]
            if self.rows > 1:
                total = both[1]
                for j in range(2, self.rows + 1):
                    total = both[j % self.rows] + self.shift(total.astype(bf16), 1).astype(f32)
            else:
                total = both[0]
            held.append(total)
        total = held[1]
        for k in range(2, RING + 1):
            total = held[k % RING] + self.shift(total.astype(bf16), 0).astype(f32)
        return total


def swap(value):
    return lax.ppermute(value, "sp", [(0, 1), (1, 0)])


def rotate(values, cosine, sine):
    rows = values.shape[0]
    parts = values.reshape(rows, -1, HEAD_DIM)
    half = HEAD_DIM // 2
    leading, trailing = parts[..., :half], parts[..., half:]
    cosine, sine = cosine[:, None, :], sine[:, None, :]
    turned = jnp.concatenate(
        [leading * cosine - trailing * sine, trailing * cosine + leading * sine], axis=-1
    )
    return turned.reshape(values.shape)


def load_pieces(count, place_ref, piece_refs, table, sems):
    copies = [
        pltpu.make_async_copy(piece_refs[i], table.at[place_ref[i]], sems.at[i])
        for i in range(count)
    ]
    for copy in copies:
        copy.start()
    for copy in copies:
        copy.wait()


def attend_kernel(count, heads, me_ref, place_ref, query_ref, *refs):
    piece_refs = refs[:count]
    out_ref, lse_ref = refs[count : count + 2]
    table, top, total, acc, sems = refs[count + 2 :]
    load_pieces(count, place_ref, piece_refs, table, sems)
    scale = HEAD_DIM**-0.5 * log2e
    top[...] = jnp.full(top.shape, masked_value, f32)
    total[...] = jnp.zeros(total.shape, f32)
    acc[...] = jnp.zeros(acc.shape, f32)

    def step(g, _):
        keys = table[g, :, :HEAD_DIM]
        values = table[g, :, HEAD_DIM:]
        for h in range(heads):
            columns = slice(h * HEAD_DIM, (h + 1) * HEAD_DIM)
            scores = dot_nt(keys, query_ref[:, columns]) * scale
            old = top[h]
            new = jnp.maximum(old, jnp.max(scores, axis=0, keepdims=True))
            probs = jnp.exp2(scores - new)
            shrink = jnp.exp2(old - new)
            top[h] = new
            total[h] = total[h] * shrink + jnp.sum(probs, axis=0, keepdims=True)
            acc[h] = acc[h] * shrink + dot_tn(values, probs.astype(bf16))
        return 0

    lax.fori_loop(0, me_ref[0] + 1, step, 0)
    for h in range(heads):
        columns = slice(h * HEAD_DIM, (h + 1) * HEAD_DIM)
        out_ref[:, columns] = (acc[h] / total[h]).T
        lse_ref[h] = top[h] + jnp.log2(total[h])


def attend(count, me, place, queries, pieces):
    rows, width = queries.shape
    heads = width // HEAD_DIM
    piece_rows, piece_width = pieces[0].shape
    smem = pl.BlockSpec(memory_space=pltpu.SMEM)
    vmem = pl.BlockSpec(memory_space=pltpu.VMEM)
    return pl.pallas_call(
        functools.partial(attend_kernel, count, heads),
        out_shape=(
            jax.ShapeDtypeStruct((rows, width), f32),
            jax.ShapeDtypeStruct((heads, 1, rows), f32),
        ),
        in_specs=[smem, smem, vmem] + [pl.BlockSpec(memory_space=pl.ANY)] * count,
        out_specs=(vmem, vmem),
        scratch_shapes=[
            pltpu.VMEM((count, piece_rows, piece_width), bf16),
            pltpu.VMEM((heads, 1, rows), f32),
            pltpu.VMEM((heads, 1, rows), f32),
            pltpu.VMEM((heads, HEAD_DIM, rows), f32),
            pltpu.SemaphoreType.DMA((count,)),
        ],
        compiler_params=pltpu.CompilerParams(vmem_limit_bytes=48 * 1024 * 1024),
        name="attend",
    )(me, place, queries, *pieces)


def attend_back_kernel(count, heads, me_ref, place_ref, spot_ref, query_ref, grad_ref, lse_ref, delta_ref, *refs):
    piece_refs = refs[:count]
    dq_ref, dkv_ref = refs[count : count + 2]
    table, sems = refs[count + 2 :]
    load_pieces(count, place_ref, piece_refs, table, sems)
    scale = HEAD_DIM**-0.5 * log2e
    dq_ref[...] = jnp.zeros(dq_ref.shape, f32)
    dkv_ref[...] = jnp.zeros(dkv_ref.shape, dkv_ref.dtype)

    def step(g, _):
        keys = table[g, :, :HEAD_DIM]
        values = table[g, :, HEAD_DIM:]
        key_sum = jnp.zeros((keys.shape[0], HEAD_DIM), f32)
        value_sum = jnp.zeros((keys.shape[0], HEAD_DIM), f32)
        for h in range(heads):
            columns = slice(h * HEAD_DIM, (h + 1) * HEAD_DIM)
            queries = query_ref[:, columns]
            grads = grad_ref[:, columns]
            probs = jnp.exp2(dot_nt(keys, queries) * scale - lse_ref[h])
            value_sum = value_sum + dot(probs.astype(bf16), grads)
            slopes = (probs * (dot_nt(values, grads) - delta_ref[h])).astype(bf16)
            key_sum = key_sum + dot(slopes, queries)
            dq_ref[:, columns] += dot_tn(slopes, keys)
        spot = spot_ref[g]
        dkv_ref[spot, :, :HEAD_DIM] = (key_sum * HEAD_DIM**-0.5).astype(dkv_ref.dtype)
        dkv_ref[spot, :, HEAD_DIM:] = value_sum.astype(dkv_ref.dtype)
        return 0

    lax.fori_loop(0, me_ref[0] + 1, step, 0)


def attend_back(count, me, place, spot, queries, grads, lse, delta, pieces):
    rows, width = queries.shape
    heads = width // HEAD_DIM
    piece_rows, piece_width = pieces[0].shape
    smem = pl.BlockSpec(memory_space=pltpu.SMEM)
    vmem = pl.BlockSpec(memory_space=pltpu.VMEM)
    return pl.pallas_call(
        functools.partial(attend_back_kernel, count, heads),
        out_shape=(
            jax.ShapeDtypeStruct((rows, width), f32),
            jax.ShapeDtypeStruct((count, piece_rows, piece_width), bf16),
        ),
        in_specs=[smem] * 3 + [vmem] * 4 + [pl.BlockSpec(memory_space=pl.ANY)] * count,
        out_specs=(vmem, vmem),
        scratch_shapes=[
            pltpu.VMEM((count, piece_rows, piece_width), bf16),
            pltpu.SemaphoreType.DMA((count,)),
        ],
        compiler_params=pltpu.CompilerParams(vmem_limit_bytes=48 * 1024 * 1024),
        name="attend_back",
    )(me, place, spot, queries, grads, lse, delta, *pieces)


def split3(values):
    high = values.astype(bf16)
    rest = values - high.astype(f32)
    middle = rest.astype(bf16)
    low = (rest - middle.astype(f32)).astype(bf16)
    return jnp.concatenate([high, middle, low], axis=1)


def gelu_product(gate_lin, up_lin):
    return jax.nn.gelu(gate_lin, approximate=True) * up_lin


def body(
    tokens,
    cotangent,
    routes,
    attn_gain,
    query_weight,
    key_matrix,
    value_matrix,
    output_weight,
    moe_gain,
    router_weight,
    gate_weight,
    up_weight,
    down_weight,
):
    rows, width = tokens.shape
    top_k = routes.shape[1]
    count = lax.axis_size("fsdp")
    me = lax.axis_index("fsdp")
    side = lax.axis_index("sp")
    plane = Plane(count)
    sources = plane.sources(me)
    spots = plane.positions(me)
    shard = query_weight.shape[0]
    half_q = query_weight.shape[1] // 2
    half_kv = key_matrix.shape[1] // 2

    pair = jnp.concatenate([tokens, swap(tokens)], axis=0)

    own_w = jnp.concatenate(
        [
            lax.dynamic_slice_in_dim(query_weight, side * half_q, half_q, 1),
            lax.dynamic_slice_in_dim(key_matrix, side * half_kv, half_kv, 1),
            lax.dynamic_slice_in_dim(value_matrix, side * half_kv, half_kv, 1),
            router_weight,
            attn_gain[:, None],
            moe_gain[:, None],
            jnp.zeros((shard, 128 - EXPERTS - 2), bf16),
        ],
        axis=1,
    )
    qkv_width = half_q + 2 * half_kv
    w_all = jnp.take(jnp.stack(plane.gather(own_w)), spots, axis=0).reshape(width, own_w.shape[1])
    w_qkv = w_all[:, :qkv_width]
    w_router = w_all[:, qkv_width : qkv_width + EXPERTS]
    gains = w_all[:, qkv_width + EXPERTS : qkv_width + EXPERTS + 2].astype(f32).T
    gain_one, gain_two = gains[0:1], gains[1:2]

    out_piece = shard // 2
    per_side = count // 2
    upper = me // per_side
    mine = lax.dynamic_slice_in_dim(
        output_weight, jnp.where(upper == side, 0, out_piece), out_piece, 0
    )
    moves = []
    for g in range(count):
        for p in range(2):
            half = g // per_side
            target = 2 * (g % per_side) + (0 if p == half else 1)
            moves.append((g * 2 + p, target * 2 + half))
    mine = lax.ppermute(mine, ("fsdp", "sp"), moves)
    w_out = jnp.take(jnp.stack(plane.gather(mine)), spots, axis=0).reshape(half_q, width)

    inputs = pair.astype(f32)
    scale_one = lax.rsqrt(jnp.mean(inputs * inputs, axis=-1, keepdims=True) + epsilon)
    normed = (inputs * scale_one * gain_one).astype(bf16)
    lin = dot(normed, w_qkv)
    steps = jnp.arange(rows, dtype=jnp.int32)
    start = me * 2 * rows
    positions = jnp.concatenate([start + side * rows + steps, start + (1 - side) * rows + steps])
    frequency = rotary_base ** (-jnp.arange(HEAD_DIM // 2).astype(f32) * 2.0 / HEAD_DIM)
    angles = positions.astype(f32)[:, None] * frequency[None, :]
    cosine, sine = jnp.cos(angles), jnp.sin(angles)
    queries = rotate(lin[:, :half_q], cosine, sine).astype(bf16)
    keys = rotate(lin[:, half_q : half_q + half_kv], cosine, sine).astype(bf16)
    packed = jnp.concatenate([keys, lin[:, half_q + half_kv :].astype(bf16)], axis=1)
    pieces = plane.gather(packed)

    experts = jnp.arange(EXPERTS, dtype=jnp.int32)
    chosen = routes[:, :, None] == experts[None, None, :]
    named = jnp.any(chosen, axis=1)
    before = (steps[:, None] > steps[None, :]).astype(bf16)
    rank = dot(before, named.astype(bf16))
    slots = jnp.where(named, rank, -1.0).T
    columns = gate_weight.shape[1]
    local = max(1, columns // FF)
    owners = max(1, FF // columns)
    wide = columns // local
    first = me * columns // FF
    all_slots = lax.all_gather(slots, "fsdp", axis=0)
    my_slots = lax.dynamic_slice_in_dim(all_slots, first, local, 1)
    my_slots = jnp.take(my_slots, sources, axis=0)
    picks = (
        my_slots[:, :, None, :] == jnp.arange(MOST, dtype=f32)[None, None, :, None]
    ).astype(bf16)
    flat_picks = picks.reshape(count, local * MOST, rows)

    cot_rows = jnp.stack(
        [dot(flat_picks[i], block).astype(bf16) for i, block in enumerate(plane.gather(cotangent))]
    )
    cot_other = swap(cot_rows)

    me_ref = me.astype(jnp.int32).reshape(1)
    attended, lse = attend(count, me_ref, sources, queries, pieces)
    heads = attended.astype(bf16)
    projected = dot(heads, w_out)
    hidden = inputs[:rows] + projected[:rows] + swap(projected[rows:].astype(bf16)).astype(f32)
    scale_two = lax.rsqrt(jnp.mean(hidden * hidden, axis=-1, keepdims=True) + epsilon)
    mixed = (hidden * scale_two * gain_two).astype(bf16)
    logits = dot(mixed, w_router)
    picked = jnp.sum(jnp.where(chosen, logits[:, None, :], 0.0), axis=-1)
    gates = jax.nn.softmax(picked, axis=-1)
    dense_gates = jnp.sum(jnp.where(chosen, gates[:, :, None], 0.0), axis=1)

    sent = jnp.concatenate(
        [mixed, split3(dense_gates), jnp.zeros((rows, 128 - 3 * EXPERTS), bf16)], axis=1
    )
    got = jnp.stack(
        [dot(flat_picks[i], block).astype(bf16) for i, block in enumerate(plane.gather(sent))]
    ).reshape(count, local, MOST, width + 128)
    got_other = swap(got)
    expert_of = (first + jnp.arange(local))[None, :, None, None]
    lanes = jnp.arange(128)[None, None, None, :]
    own_gate = (lanes < 3 * EXPERTS) & (lanes % EXPERTS == expert_of)

    def gates_of(rows_in):
        return jnp.sum(
            jnp.where(own_gate, rows_in[..., width:].astype(f32), 0.0), axis=-1, keepdims=True
        )

    gate_cols = gate_weight.reshape(width, local, wide)
    up_cols = up_weight.reshape(width, local, wide)
    down_rows = down_weight.reshape(local, wide, width)

    def hidden_units(rows_in, cot_in):
        x = rows_in[..., :width]
        route_grad = (gates_of(rows_in) * cot_in.astype(f32)).astype(bf16)
        gate_lin = jnp.einsum("sgmd,dgc->sgmc", x, gate_cols, preferred_element_type=f32)
        up_lin = jnp.einsum("sgmd,dgc->sgmc", x, up_cols, preferred_element_type=f32)
        inner, back = jax.vjp(gelu_product, gate_lin, up_lin)
        inner_grad = jnp.einsum(
            "sgmd,gcd->sgmc", route_grad, down_rows, preferred_element_type=f32
        )
        gate_d, up_d = back(inner_grad)
        return x, route_grad, inner.astype(bf16), gate_d.astype(bf16), up_d.astype(bf16)

    cot_rows = cot_rows.reshape(count, local, MOST, width)
    cot_other = cot_other.reshape(count, local, MOST, width)
    here = hidden_units(got, cot_rows)
    x, route_grad, inner, gate_d, up_d = here
    expert_out = jnp.einsum("sgmc,gcd->sgmd", inner, down_rows, preferred_element_type=f32)
    gate_dot = jnp.sum(expert_out * cot_rows.astype(f32), axis=-1)
    mixed_part = jnp.einsum("sgmc,dgc->sgmd", gate_d, gate_cols, preferred_element_type=f32)
    mixed_part = mixed_part + jnp.einsum(
        "sgmc,dgc->sgmd", up_d, up_cols, preferred_element_type=f32
    )

    def home(values):
        flat = values.astype(bf16).reshape(RING, plane.rows, CORES, local * MOST, width)
        pick = flat_picks.reshape(RING, plane.rows, CORES, local * MOST, rows)
        parts = [
            [
                jnp.einsum("jst,jsd->jtd", pick[k, :, m], flat[k, :, m], preferred_element_type=f32)
                .astype(bf16)
                for m in range(CORES)
            ]
            for k in range(RING)
        ]
        return plane.scatter(parts)

    mixed_grad = home(mixed_part)
    mixture = home(gates_of(got) * expert_out)
    output = (hidden + mixture).astype(bf16)

    slot_dots = jnp.sum(
        jnp.where(picks > 0, gate_dot[:, :, :, None], 0.0), axis=2
    )
    slot_dots = jnp.take(slot_dots, spots, axis=0)
    slot_dots = lax.all_to_all(slot_dots, "fsdp", split_axis=0, concat_axis=0, tiled=True)
    slot_dots = slot_dots.reshape(EXPERTS, owners, rows).sum(axis=1).T
    gate_grad_k = jnp.sum(jnp.where(chosen, slot_dots[:, None, :], 0.0), axis=-1)
    picked_grad = gates * (gate_grad_k - jnp.sum(gates * gate_grad_k, axis=-1, keepdims=True))
    logit_grad = jnp.sum(jnp.where(chosen, picked_grad[:, :, None], 0.0), axis=1).astype(bf16)
    router_part = dot_tn(mixed, logit_grad)
    mixed_grad = mixed_grad + dot_nt(logit_grad, w_router)

    out_grad = cotangent.astype(f32)
    moe_gain_part = jnp.sum(mixed_grad * hidden * scale_two, axis=0)
    weighted = mixed_grad * gain_two
    hidden_grad = (
        out_grad
        + scale_two * weighted
        - hidden * scale_two**3 * jnp.mean(hidden * weighted, axis=-1, keepdims=True)
    )
    attn_grad = hidden_grad.astype(bf16)
    attn_grad = jnp.concatenate([attn_grad, swap(attn_grad)], axis=0)
    heads_grad = dot_nt(attn_grad, w_out).astype(bf16)
    output_part = dot_tn(heads, attn_grad)
    head_count = half_q // HEAD_DIM
    delta = jnp.sum(
        (heads_grad.astype(f32) * attended).reshape(2 * rows, head_count, HEAD_DIM), axis=-1
    ).T.reshape(head_count, 1, 2 * rows)
    query_sum, kv_part = attend_back(
        count, me_ref, sources, spots, queries, heads_grad, lse, delta, pieces
    )
    kv_part = kv_part.reshape(RING, plane.rows, CORES, 2 * rows, 2 * half_kv)
    kv_grad = plane.scatter(
        [[kv_part[k, :, m] for m in range(CORES)] for k in range(RING)]
    ).astype(bf16)
    query_out = (query_sum * HEAD_DIM**-0.5).astype(bf16)
    query_lin = rotate(query_out.astype(f32), cosine, -sine).astype(bf16)
    key_lin = rotate(kv_grad[:, :half_kv].astype(f32), cosine, -sine).astype(bf16)
    lin_grad = jnp.concatenate([query_lin, key_lin, kv_grad[:, half_kv:]], axis=1)
    normed_part = dot_nt(lin_grad, w_qkv)
    normed_grad = normed_part[:rows] + swap(normed_part[rows:].astype(bf16)).astype(f32)
    weighted = normed_grad * gain_one
    own, own_scale = inputs[:rows], scale_one[:rows]
    input_grad = (
        hidden_grad
        + own_scale * weighted
        - own * own_scale**3 * jnp.mean(own * weighted, axis=-1, keepdims=True)
    ).astype(bf16)
    attn_gain_part = jnp.sum(normed_part * inputs * scale_one, axis=0)

    qkv_part = dot_tn(normed, lin_grad)
    weight_part = jnp.concatenate(
        [
            qkv_part,
            router_part,
            attn_gain_part[:, None],
            moe_gain_part[:, None],
            jnp.zeros((width, 128 - EXPERTS - 2), f32),
        ],
        axis=1,
    ).astype(bf16)

    def shards(values):
        blocks = jnp.take(
            values.reshape(count, values.shape[0] // count, values.shape[1]), sources, axis=0
        )
        blocks = blocks.reshape((RING, plane.rows, CORES) + blocks.shape[1:])
        return plane.scatter([[blocks[k, :, m] for m in range(CORES)] for k in range(RING)])

    weight_shard = shards(weight_part).astype(bf16)
    weight_other = swap(weight_shard).astype(f32)
    weight_shard = weight_shard.astype(f32)
    low = jnp.where(side == 0, weight_shard, weight_other)
    high = jnp.where(side == 0, weight_other, weight_shard)
    query_grad = jnp.concatenate([low[:, :half_q], high[:, :half_q]], axis=1)
    cut = half_q + half_kv
    key_grad = jnp.concatenate([low[:, half_q:cut], high[:, half_q:cut]], axis=1)
    value_grad = jnp.concatenate([low[:, cut:qkv_width], high[:, cut:qkv_width]], axis=1)
    tail = weight_shard[:, qkv_width:] + weight_other[:, qkv_width:]
    router_grad = tail[:, :EXPERTS]
    attn_gain_grad = tail[:, EXPERTS]
    moe_gain_grad = tail[:, EXPERTS + 1]

    out_shard = shards(output_part.astype(bf16)).astype(bf16)
    out_shard = lax.ppermute(out_shard, ("fsdp", "sp"), [(b, a) for a, b in moves])
    out_other = swap(out_shard)
    output_grad = jnp.where(
        upper == side,
        jnp.concatenate([out_shard, out_other], axis=0),
        jnp.concatenate([out_other, out_shard], axis=0),
    ).astype(f32)

    there = hidden_units(got_other, cot_other)

    def both(pattern, left, right):
        return sum(
            jnp.einsum(pattern, part[left], part[right], preferred_element_type=f32)
            for part in (here, there)
        )

    down_grad = both("sgmc,sgmd->gcd", 2, 1).reshape(columns, width)
    gate_grad = both("sgmd,sgmc->dgc", 0, 3).reshape(width, columns)
    up_grad = both("sgmd,sgmc->dgc", 0, 4).reshape(width, columns)

    return (
        output,
        input_grad,
        query_grad,
        key_grad,
        value_grad,
        output_grad,
        router_grad,
        gate_grad,
        up_grad,
        down_grad,
        attn_gain_grad,
        moe_gain_grad,
    )


def solution(mesh):
    token = P(("fsdp", "sp"), None)
    in_specs = (
        token,
        token,
        token,
        P("fsdp"),
        P("fsdp", None),
        P("fsdp", None),
        P("fsdp", None),
        P("fsdp", None),
        P("fsdp"),
        P("fsdp", None),
        P(None, "fsdp"),
        P(None, "fsdp"),
        P("fsdp", None),
    )
    out_specs = (
        token,
        token,
        P("fsdp", None),
        P("fsdp", None),
        P("fsdp", None),
        P("fsdp", None),
        P("fsdp", None),
        P(None, "fsdp"),
        P(None, "fsdp"),
        P("fsdp", None),
        P("fsdp"),
        P("fsdp"),
    )
    return jax.shard_map(body, mesh=mesh, in_specs=in_specs, out_specs=out_specs, check_vma=False)
```

time: 1810 us -> 872 us (0.48)
  waiting for transfers between devices: 1130 us -> 353 us
  blocking collectives: 302 us -> 21.5 us
  starting transfers between devices: 42.8 us -> 115 us
  matrix products: 102 us -> 170 us
  other arithmetic: 88 us -> 51.2 us
    psum x1 -> x0, waiting for transfers between devices: 567 us -> none  [pair_sum(): lax.psum(query_g.astype(jnp.bfloat16), 'sp').astype(jnp.float32)]
    reduce_scatter x5 -> x0, waiting for transfers between devices: 403 us -> none  [the longest x1 116 us: shard_sum(): lax.psum_scatter(output_g, 'fsdp', scatter_dimension=0, tiled=True)]
    ppermute x0 -> x140, waiting for transfers between devices: none -> 353 us  [the longest x130 264 us: shift(): return lax.ppermute(value, 'fsdp', self.along(which))]
    ppermute x0 -> x140, starting transfers between devices: none -> 112 us  [the longest x130 100 us: shift(): return lax.ppermute(value, 'fsdp', self.along(which))]
    all_to_all x8 -> x1, waiting for transfers between devices: 98.7 us -> 0.01 us  [body(): lax.all_to_all(slot_dots, 'fsdp', split_axis=0, concat_axis=0, tiled=True)]
    unnamed x2 -> x0, blocking collectives: 96.7 us -> none
    all_to_all x2 -> x0, blocking collectives: 93.6 us -> none  [the longest x1 86.6 us: body(): lax.all_to_all(jnp.take(padded_grad, slot_table, axis=0), 'fsdp', split_a...]
    all_gather x3 -> x1, blocking collectives: 107 us -> 21.5 us  [body(): all_slots = lax.all_gather(slots, 'fsdp', axis=0)]
  transfers between devices with their start and end apart: 18 -> 141, of which waited for: 13 -> 50; matrix products, arithmetic and copies ran while one was open for 9% -> 37% of each run, Pallas kernels for 0% -> 1%
where the time goes in v1:
time: 872 us; the launch traced here: 861 us
  waiting for transfers between devices  353 us (40%)
  matrix products  170 us (19%)
  local copies, waits for them, and re-layouts  134 us (15%)
  starting transfers between devices  115 us (13%)
  other arithmetic  51.2 us (6%)
  blocking collectives  21.5 us (2%)
  Pallas kernels  11.9 us (1%)
    ppermute x130, waiting for transfers between devices, shift(): return lax.ppermute(value, 'fsdp', self.along(which))  264 us
    ppermute x130, starting transfers between devices, shift(): return lax.ppermute(value, 'fsdp', self.along(which))  100 us
    ppermute x8, waiting for transfers between devices, swap(): return lax.ppermute(value, 'sp', [(0, 1), (1, 0)])  89 us
    unnamed x389, local copies, waits for them, and re-layouts  69.7 us
    dot_general x6, matrix products, both(): jnp.einsum(pattern, part[left], part[right], preferred_element_type=f32)  54.8 us
    dot_general x36, matrix products, dot(): return jnp.dot(a, b, preferred_element_type=f32)  34.9 us
    all_gather x1, blocking collectives, body(): all_slots = lax.all_gather(slots, 'fsdp', axis=0)  21.5 us
    dot_general x16, matrix products, home(): jnp.einsum('jst,jsd->jtd', pick[k, :, m], flat[k, :, m], preferred_elemen...  21 us
  transfers between devices with their start and end apart: 141, of which 50 were waited for; matrix products, arithmetic and copies ran while one was open for 37% of the time, Pallas kernels for 1%

profile of v1, /device:TPU:0, one launch (start us, length us, event | category | flops | bytes accessed | tf_op | source)
XLA Modules:
  0.0 860.8 jit_solution(7317892438984837149)
XLA Ops:
  14.0 21.5 %all-gather = f32[512,128]{1,0:T(8,128)S(1)} all-gather(f32[32,128]{1,0:T(8,128)S(1)} %convolution_select_fusion), channel_id=2, replica_groups=mesh['fsdp'=16,'sp'=2] {'fsdp'}, dimensions={0}, use_global_device_ids=true | all-gather | bytes 278528 | tf_op jit(solution)/shard_map/all_gather | solution.py:356
  38.7 10.6 %reshape.808 = bf16[1536,2,768]{2,1,0:T(2,128)(2,1)} reshape(bf16[1536,1536]{1,0:T(8,128)(2,1)} %param.29) | data formatting | bytes 9437184 | tf_op jit(solution)/shard_map/reshape | solution.py:397
  49.3 10.7 %reshape.809 = bf16[1536,2,768]{2,1,0:T(2,128)(2,1)} reshape(bf16[1536,1536]{1,0:T(8,128)(2,1)} %param.30) | data formatting | bytes 9437184 | tf_op jit(solution)/shard_map/reshape | solution.py:398
  68.1 9.0 %collective-permute-done.33 = bf16[48,1536]{1,0:T(8,128)(2,1)S(1)} collective-permute-done((bf16[48,1536]{1,0:T(8,128)(2,1)S(1)}, bf16[48,1536]{1,0:T(8,128)(2,1)S(1)}, u32[]{:S(2)}, u32[]{:S(2)}) %collective-permute-start.33) | collective-permute-done | bytes 147488 | tf_op jit(solution)/shard_map/ppermute | solution.py:82
  78.1 9.5 %collective-permute-done = bf16[128,1536]{1,0:T(8,128)(2,1)S(1)} collective-permute-done((bf16[128,1536]{1,0:T(8,128)(2,1)S(1)}, bf16[128,1536]{1,0:T(8,128)(2,1)S(1)}, u32[]{:S(2)}, u32[]{:S(2)}) %collective-permute-start) | collective-permute-done | bytes 393248 | tf_op jit(solution)/shard_map/ppermute | solution.py:117
  105.8 5.6 collective-permute-done.39
  114.8 10.7 %collective-permute-done.41 = bf16[48,1536]{1,0:T(8,128)(2,1)S(1)} collective-permute-done((bf16[48,1536]{1,0:T(8,128)(2,1)S(1)}, bf16[48,1536]{1,0:T(8,128)(2,1)S(1)}, u32[]{:S(2)}, u32[]{:S(2)}) %collective-permute-start.41) | collective-permute-done | bytes 147488 | tf_op jit(solution)/shard_map/ppermute | solution.py:82
  130.8 5.5 collective-permute-done.10
  140.5 4.4 collective-permute-done.45
  145.6 9.4 %collective-permute-done.12 = bf16[96,1152]{1,0:T(8,128)(2,1)S(1)} collective-permute-done((bf16[96,1152]{1,0:T(8,128)(2,1)S(1)}, bf16[96,1152]{1,0:T(8,128)(2,1)S(1)}, u32[]{:S(2)}, u32[]{:S(2)}) %collective-permute-start.12) | collective-permute-done | bytes 221216 | tf_op jit(solution)/shard_map/ppermute | solution.py:82
  175.9 4.9 gather_fusion
  206.5 3.4 collective-permute-done.19.refs_4_
  211.6 5.1 collective-permute-done.23.refs_8_
  219.7 3.8 collective-permute-done.27.refs_12_
  225.4 5.5 collective-permute-done.25.refs_10_
  233.6 5.9 attend.1
  244.4 6.9 collective-permute-done.47
  257.2 4.4 collective-permute-start.49
  261.6 7.6 collective-permute-start.51
  272.6 24.1 %collective-permute-done.51 = bf16[128,1664]{1,0:T(8,128)(2,1)S(1)} collective-permute-done((bf16[128,1664]{1,0:T(8,128)(2,1)S(1)}, bf16[128,1664]{1,0:T(8,128)(2,1)S(1)}, u32[]{:S(2)}, u32[]{:S(2)}) %collective-permute-start.51) | collective-permute-done | bytes 426016 | tf_op jit(solution)/shard_map/ppermute | solution.py:82
  299.3 9.6 %collective-permute-done.53 = bf16[128,1664]{1,0:T(8,128)(2,1)S(1)} collective-permute-done((bf16[128,1664]{1,0:T(8,128)(2,1)S(1)}, bf16[128,1664]{1,0:T(8,128)(2,1)S(1)}, u32[]{:S(2)}, u32[]{:S(2)}) %collective-permute-start.53) | collective-permute-done | bytes 426016 | tf_op jit(solution)/shard_map/ppermute | solution.py:82
  313.8 14.7 %collective-permute-start.59 = (bf16[128,1664]{1,0:T(8,128)(2,1)S(1)}, bf16[128,1664]{1,0:T(8,128)(2,1)S(1)}, u32[]{:S(2)}, u32[]{:S(2)}) collective-permute-start(bf16[128,1664]{1,0:T(8,128)(2,1)S(1)} %collective-permute-done.55), channel_id=1, source_target_pairs={{0,8},{2,10},{4,12},{6,14},{8,16},{10,18},{12,20},{14,22},{16,24},... | collective-permute-start | bytes 1277960 | tf_op jit(solution)/shard_map/ppermute | solution.py:82
  329.5 12.7 %collective-permute-done.59 = bf16[128,1664]{1,0:T(8,128)(2,1)S(1)} collective-permute-done((bf16[128,1664]{1,0:T(8,128)(2,1)S(1)}, bf16[128,1664]{1,0:T(8,128)(2,1)S(1)}, u32[]{:S(2)}, u32[]{:S(2)}) %collective-permute-start.59) | collective-permute-done | bytes 426016 | tf_op jit(solution)/shard_map/ppermute | solution.py:82
  343.0 11.4 %collective-permute-done.61 = bf16[128,1664]{1,0:T(8,128)(2,1)S(1)} collective-permute-done((bf16[128,1664]{1,0:T(8,128)(2,1)S(1)}, bf16[128,1664]{1,0:T(8,128)(2,1)S(1)}, u32[]{:S(2)}, u32[]{:S(2)}) %collective-permute-start.61) | collective-permute-done | bytes 426016 | tf_op jit(solution)/shard_map/ppermute | solution.py:82
  367.1 4.3 fusion.13
  371.4 4.3 fusion.7
  375.7 57.3 %collective-permute-done.138 = bf16[16,2,32,1664]{3,2,0,1:T(8,128)(2,1)S(1)} collective-permute-done((bf16[16,2,32,1664]{3,2,0,1:T(8,128)(2,1)S(1)}, bf16[16,2,32,1664]{3,2,0,1:T(8,128)(2,1)S(1)}, u32[]{:S(2)}, u32[]{:S(2)}) %collective-permute-start.138) | collective-permute-done | bytes 3407904 | tf_op jit(solution)/shard_map/ppermute | solution.py:117
  434.9 9.2 %fusion.36 = (bf16[16,2,32,768]{3,2,0,1:T(8,128)(2,1)S(1)}, bf16[16,2,32,768]{3,2,0,1:T(8,128)(2,1)S(1)}, bf16[16,2,32,768]{3,2,0,1:T(8,128)(2,1)}) fusion(f32[2,16,32,768]{3,2,1,0:T(8,128)} %fusion.13, f32[2,16,32,768]{3,2,1,0:T(8,128)} %fusion.7, bf16[2,768,1536,1]{2,1,3,0:T(8,128)(2,1)} %bitcast.1023, bf16[16,2,32,1536]{3,2,0,1:T(8,128)(2,1)S(1)} %copy-done.129, ...), kind=kOutput, calls=%fused_computation.63 | convolution fusion | flops 2441084928 | bytes 18878464 | tf_op jit(solution)/shard_map/sgmd,gcd->sgmc/dot_general | solution.py:407
  444.1 4.6 fusion.11
  448.7 4.9 fusion.15
  479.3 3.5 all-to-all-start
  483.2 8.9 %fusion.54 = f32[2,768,1536,1]{2,1,3,0:T(8,128)} fusion(bf16[16,2,32,768]{3,2,0,1:T(8,128)(2,1)} %copy-done.144, bf16[16,2,32,1664]{3,2,0,1:T(8,128)(2,1)} %copy-done.112), kind=kOutput, calls=%fused_computation.133 | convolution fusion | flops 2415919104 | bytes 14155776 | tf_op jit(solution)/shard_map/sgmd,sgmc->dgc/dot_general | solution.py:537
  492.2 5.7 fusion.44
  499.8 6.4 fusion.68
  508.9 4.3 fusion.4
  513.2 12.6 %bitcast_add_fusion = f32[2,768,1536]{2,1,0:T(8,128)} fusion(f32[2,768,1536,1]{2,1,3,0:T(8,128)} %fusion.44, f32[2,16,32,768]{3,2,1,0:T(8,128)} %fusion.4, f32[2,16,32,768]{3,2,1,0:T(8,128)S(1)} %fusion.9, f32[16,2,32]{2,0,1:T(8,128)S(1)} %get-tuple-element.101, bf16[16,2,32,1536]{3,2,1,0:T(8,128)(2,1)} %bitcast.362), kind=kOutput, calls=%fused_computation.6 | convolution fusion | flops 2430861312 | bytes 28315648 | tf_op jit(solution)/shard_map/sgmc,sgmd->gcd/dot_general | solution.py:537
  525.8 14.6 %bitcast_add_fusion.2 = f32[2,768,1536]{2,1,0:T(8,128)} fusion(f32[2,768,1536,1]{2,1,3,0:T(8,128)} %fusion.54, bf16[16,2,32,1664]{3,2,0,1:T(8,128)(2,1)S(1)} %copy-done.118, f32[2,16,32,768]{3,2,1,0:T(8,128)} %copy-done.146, f32[2,16,32,768]{3,2,1,0:T(8,128)} %fusion.4, f32[2,16,32,768]{3,2,1,0:T(8,128)} %fusion.68), kind=kOutput, calls=%fused_computation.8 | convolution fusion | flops 2434793472 | bytes 31457280 | tf_op jit(solution)/shard_map/sgmd,sgmc->dgc/dot_general | solution.py:537
  556.8 3.7 collective-permute-done.96
  562.0 32.2 %collective-permute-done.70 = bf16[128,1536]{1,0:T(8,128)(2,1)S(1)} collective-permute-done((bf16[128,1536]{1,0:T(8,128)(2,1)S(1)}, bf16[128,1536]{1,0:T(8,128)(2,1)S(1)}, u32[]{:S(2)}, u32[]{:S(2)}) %collective-permute-start.70) | collective-permute-done | bytes 393248 | tf_op jit(solution)/shard_map/ppermute | solution.py:82
  596.8 8.9 %collective-permute-done.97 = bf16[128,1536]{1,0:T(8,128)(2,1)S(1)} collective-permute-done((bf16[128,1536]{1,0:T(8,128)(2,1)S(1)}, bf16[128,1536]{1,0:T(8,128)(2,1)S(1)}, u32[]{:S(2)}, u32[]{:S(2)}) %collective-permute-start.97) | collective-permute-done | bytes 393248 | tf_op jit(solution)/shard_map/ppermute | solution.py:82
  606.3 9.8 %collective-permute-done.71 = bf16[128,1536]{1,0:T(8,128)(2,1)S(1)} collective-permute-done((bf16[128,1536]{1,0:T(8,128)(2,1)S(1)}, bf16[128,1536]{1,0:T(8,128)(2,1)S(1)}, u32[]{:S(2)}, u32[]{:S(2)}) %collective-permute-start.71) | collective-permute-done | bytes 393248 | tf_op jit(solution)/shard_map/ppermute | solution.py:82
  616.5 13.5 %collective-permute-done.98 = bf16[128,1536]{1,0:T(8,128)(2,1)S(1)} collective-permute-done((bf16[128,1536]{1,0:T(8,128)(2,1)S(1)}, bf16[128,1536]{1,0:T(8,128)(2,1)S(1)}, u32[]{:S(2)}, u32[]{:S(2)}) %collective-permute-start.98) | collective-permute-done | bytes 393248 | tf_op jit(solution)/shard_map/ppermute | solution.py:82
  630.4 8.1 collective-permute-done.72
  638.8 8.1 collective-permute-done.99
  653.6 5.2 fusion.52
  661.5 3.4 convert_multiply_fusion.2
  678.9 6.0 attend_back.1
  690.2 3.2 convolution_convert_fusion.1
  693.4 4.0 gather_fusion.5
  700.8 4.1 collective-permute-start.108
  710.3 6.0 collective-permute-start.109
  718.1 17.8 %collective-permute-done.109 = bf16[256,256]{1,0:T(8,128)(2,1)S(1)} collective-permute-done((bf16[256,256]{1,0:T(8,128)(2,1)S(1)}, bf16[256,256]{1,0:T(8,128)(2,1)S(1)}, u32[]{:S(2)}, u32[]{:S(2)}) %collective-permute-start.109) | collective-permute-done | bytes 131104 | tf_op jit(solution)/shard_map/ppermute | solution.py:82
  752.2 5.1 collective-permute-done.111
  758.4 4.3 multiply_reduce_fusion
  767.4 5.8 concatenate.86
  773.3 3.2 gather_fusion.4
  783.4 4.4 collective-permute-done.135
  794.9 7.7 bitcast_add_fusion.1
  802.7 9.6 %copy.435 = f32[1536,1536]{1,0:T(8,128)} copy(f32[1536,1536]{0,1:T(8,128)} %bitcast.915) | data formatting | bytes 18874368
  812.2 9.7 %copy.436 = f32[1536,1536]{1,0:T(8,128)} copy(f32[1536,1536]{0,1:T(8,128)} %bitcast.916) | data formatting | bytes 18874368
  827.5 9.0 %collective-permute-done.137 = bf16[48,1536]{1,0:T(8,128)(2,1)S(1)} collective-permute-done((bf16[48,1536]{1,0:T(8,128)(2,1)}, bf16[48,1536]{1,0:T(8,128)(2,1)S(1)}, u32[]{:S(2)}, u32[]{:S(2)}) %collective-permute-start.137) | collective-permute-done | bytes 147488 | tf_op jit(solution)/shard_map/ppermute | solution.py:117
  841.8 3.6 collective-permute-done.114
  845.5 4.0 collective-permute-done.123
  852.3 4.3 collective-permute-done.124
  (845 shorter events, 294.7 us)
Async XLA Ops:
  4.0 58.6 %collective-permute-start.1 = (bf16[96,1152]{1,0:T(8,128)(2,1)S(1)}, bf16[96,1152]{1,0:T(8,128)(2,1)}, u32[]{:S(2)}, u32[]{:S(2)}) collective-permute-start(bf16[96,1152]{1,0:T(8,128)(2,1)S(1)} %concatenate.72), channel_id=1, source_target_pairs={{0,2},{2,0},{4,6},{6,4},{8,10},{10,8},{12,14},{14,12},{16,18},{18,... | collective-permute-start | bytes 663560 | tf_op jit(solution)/shard_map/ppermute | solution.py:82
  4.5 59.8 %collective-permute-start.2 = (bf16[96,1152]{1,0:T(8,128)(2,1)S(1)}, bf16[96,1152]{1,0:T(8,128)(2,1)}, u32[]{:S(2)}, u32[]{:S(2)}) collective-permute-start(bf16[96,1152]{1,0:T(8,128)(2,1)S(1)} %concatenate.72), channel_id=1, source_target_pairs={{0,4},{2,6},{4,0},{6,2},{8,12},{10,14},{12,8},{14,10},{16,20},{18,... | collective-permute-start | bytes 663560 | tf_op jit(solution)/shard_map/ppermute | solution.py:82
  7.1 80.8 %collective-permute-start.4 = (bf16[96,1152]{1,0:T(8,128)(2,1)S(1)}, bf16[96,1152]{1,0:T(8,128)(2,1)}, u32[]{:S(2)}, u32[]{:S(2)}) collective-permute-start(bf16[96,1152]{1,0:T(8,128)(2,1)S(1)} %concatenate.72), channel_id=1, source_target_pairs={{0,8},{2,10},{4,12},{6,14},{8,16},{10,18},{12,20},{14,22},{16,24},... | collective-permute-start | bytes 663560 | tf_op jit(solution)/shard_map/ppermute | solution.py:82
  9.6 52.9 %collective-permute-start.31 = (bf16[48,1536]{1,0:T(8,128)(2,1)S(1)}, bf16[48,1536]{1,0:T(8,128)(2,1)S(1)}, u32[]{:S(2)}, u32[]{:S(2)}) collective-permute-start(bf16[48,1536]{1,0:T(8,128)(2,1)S(1)} %constant_dynamic-slice_fusion.1), channel_id=1, source_target_pairs={{0,0},{1,2},{2,4},{3,6},{4,8},{5,10},{6,12},{7,14},{8,16},{9,18},{... | collective-permute-start | bytes 442376 | tf_op jit(solution)/shard_map/ppermute | solution.py:327
  10.3 77.7 %collective-permute-start.74 = (bf16[128,1536]{1,0:T(8,128)(2,1)}, bf16[128,1536]{1,0:T(8,128)(2,1)}, u32[]{:S(2)}, u32[]{:S(2)}) collective-permute-start(bf16[128,1536]{1,0:T(8,128)(2,1)} %param.20), channel_id=1, source_target_pairs={{0,2},{2,0},{4,6},{6,4},{8,10},{10,8},{12,14},{14,12},{16,18},{18,... | collective-permute-start | bytes 1179656 | tf_op jit(solution)/shard_map/ppermute | solution.py:82
  62.6 28.5 %collective-permute-start.75 = (bf16[128,1536]{1,0:T(8,128)(2,1)S(1)}, bf16[128,1536]{1,0:T(8,128)(2,1)S(1)}, u32[]{:S(2)}, u32[]{:S(2)}) collective-permute-start(bf16[128,1536]{1,0:T(8,128)(2,1)S(1)} %copy-done.65), channel_id=1, source_target_pairs={{0,4},{2,6},{4,0},{6,2},{8,12},{10,14},{12,8},{14,10},{16,20},{18,... | collective-permute-start | bytes 1179656 | tf_op jit(solution)/shard_map/ppermute | solution.py:82
  62.6 38.8 %collective-permute-start.77 = (bf16[128,1536]{1,0:T(8,128)(2,1)S(1)}, bf16[128,1536]{1,0:T(8,128)(2,1)S(1)}, u32[]{:S(2)}, u32[]{:S(2)}) collective-permute-start(bf16[128,1536]{1,0:T(8,128)(2,1)S(1)} %copy-done.65), channel_id=1, source_target_pairs={{0,8},{2,10},{4,12},{6,14},{8,16},{10,18},{12,20},{14,22},{16,24},... | collective-permute-start | bytes 1179656 | tf_op jit(solution)/shard_map/ppermute | solution.py:82
  98.1 27.4 %collective-permute-start.8 = (bf16[96,1152]{1,0:T(8,128)(2,1)}, bf16[96,1152]{1,0:T(8,128)(2,1)S(1)}, u32[]{:S(2)}, u32[]{:S(2)}) collective-permute-start(bf16[96,1152]{1,0:T(8,128)(2,1)} %collective-permute-done.4), channel_id=1, source_target_pairs={{0,8},{2,10},{4,12},{6,14},{8,16},{10,18},{12,20},{14,22},{16,24},... | collective-permute-start | bytes 663560 | tf_op jit(solution)/shard_map/ppermute | solution.py:82
  101.4 53.6 %collective-permute-start.76 = (bf16[128,1536]{1,0:T(8,128)(2,1)S(1)}, bf16[128,1536]{1,0:T(8,128)(2,1)S(1)}, u32[]{:S(2)}, u32[]{:S(2)}) collective-permute-start(bf16[128,1536]{1,0:T(8,128)(2,1)S(1)} %collective-permute-done.75), channel_id=1, source_target_pairs={{0,2},{2,0},{4,6},{6,4},{8,10},{10,8},{12,14},{14,12},{16,18},{18,... | collective-permute-start | bytes 1179656 | tf_op jit(solution)/shard_map/ppermute | solution.py:82
  104.6 54.1 %collective-permute-start.78 = (bf16[128,1536]{1,0:T(8,128)(2,1)S(1)}, bf16[128,1536]{1,0:T(8,128)(2,1)S(1)}, u32[]{:S(2)}, u32[]{:S(2)}) collective-permute-start(bf16[128,1536]{1,0:T(8,128)(2,1)S(1)} %collective-permute-done.77), channel_id=1, source_target_pairs={{0,2},{2,0},{4,6},{6,4},{8,10},{10,8},{12,14},{14,12},{16,18},{18,... | collective-permute-start | bytes 1179656 | tf_op jit(solution)/shard_map/ppermute | solution.py:82
  111.4 49.7 %collective-permute-start.79 = (bf16[128,1536]{1,0:T(8,128)(2,1)S(1)}, bf16[128,1536]{1,0:T(8,128)(2,1)}, u32[]{:S(2)}, u32[]{:S(2)}) collective-permute-start(bf16[128,1536]{1,0:T(8,128)(2,1)S(1)} %collective-permute-done.77), channel_id=1, source_target_pairs={{0,4},{2,6},{4,0},{6,2},{8,12},{10,14},{12,8},{14,10},{16,20},{18,... | collective-permute-start | bytes 1179656 | tf_op jit(solution)/shard_map/ppermute | solution.py:82
  136.9 27.4 %collective-permute-start.81 = (bf16[128,1536]{1,0:T(8,128)(2,1)S(1)}, bf16[128,1536]{1,0:T(8,128)(2,1)}, u32[]{:S(2)}, u32[]{:S(2)}) collective-permute-start(bf16[128,1536]{1,0:T(8,128)(2,1)S(1)} %collective-permute-done.77), channel_id=1, source_target_pairs={{0,8},{2,10},{4,12},{6,14},{8,16},{10,18},{12,20},{14,22},{16,24},... | collective-permute-start | bytes 1179656 | tf_op jit(solution)/shard_map/ppermute | solution.py:82
  155.0 14.2 %collective-permute-start.11 = (bf16[96,1152]{1,0:T(8,128)(2,1)S(1)}, bf16[96,1152]{1,0:T(8,128)(2,1)}, u32[]{:S(2)}, u32[]{:S(2)}) collective-permute-start(bf16[96,1152]{1,0:T(8,128)(2,1)S(1)} %collective-permute-done.10), channel_id=1, source_target_pairs={{0,2},{2,0},{4,6},{6,4},{8,10},{10,8},{12,14},{14,12},{16,18},{18,... | collective-permute-start | bytes 663560 | tf_op jit(solution)/shard_map/ppermute | solution.py:82
  155.0 17.3 %collective-permute-start.13 = (bf16[96,1152]{1,0:T(8,128)(2,1)S(1)}, bf16[96,1152]{1,0:T(8,128)(2,1)S(1)}, u32[]{:S(2)}, u32[]{:S(2)}) collective-permute-start(bf16[96,1152]{1,0:T(8,128)(2,1)S(1)} %collective-permute-done.12), channel_id=1, source_target_pairs={{0,2},{2,0},{4,6},{6,4},{8,10},{10,8},{12,14},{14,12},{16,18},{18,... | collective-permute-start | bytes 663560 | tf_op jit(solution)/shard_map/ppermute | solution.py:82
  158.7 13.9 %collective-permute-start.14 = (bf16[96,1152]{1,0:T(8,128)(2,1)S(1)}, bf16[96,1152]{1,0:T(8,128)(2,1)}, u32[]{:S(2)}, u32[]{:S(2)}) collective-permute-start(bf16[96,1152]{1,0:T(8,128)(2,1)S(1)} %collective-permute-done.12), channel_id=1, source_target_pairs={{0,4},{2,6},{4,0},{6,2},{8,12},{10,14},{12,8},{14,10},{16,20},{18,... | collective-permute-start | bytes 663560 | tf_op jit(solution)/shard_map/ppermute | solution.py:82
  164.4 33.2 %collective-permute-start.80 = (bf16[128,1536]{1,0:T(8,128)(2,1)}, bf16[128,1536]{1,0:T(8,128)(2,1)}, u32[]{:S(2)}, u32[]{:S(2)}) collective-permute-start(bf16[128,1536]{1,0:T(8,128)(2,1)} %collective-permute-done.79), channel_id=1, source_target_pairs={{0,2},{2,0},{4,6},{6,4},{8,10},{10,8},{12,14},{14,12},{16,18},{18,... | collective-permute-start | bytes 1179656 | tf_op jit(solution)/shard_map/ppermute | solution.py:82
  164.9 37.8 %collective-permute-start.82 = (bf16[128,1536]{1,0:T(8,128)(2,1)}, bf16[128,1536]{1,0:T(8,128)(2,1)}, u32[]{:S(2)}, u32[]{:S(2)}) collective-permute-start(bf16[128,1536]{1,0:T(8,128)(2,1)} %collective-permute-done.81), channel_id=1, source_target_pairs={{0,2},{2,0},{4,6},{6,4},{8,10},{10,8},{12,14},{14,12},{16,18},{18,... | collective-permute-start | bytes 1179656 | tf_op jit(solution)/shard_map/ppermute | solution.py:82
  169.2 35.4 %collective-permute-start.83 = (bf16[128,1536]{1,0:T(8,128)(2,1)}, bf16[128,1536]{1,0:T(8,128)(2,1)}, u32[]{:S(2)}, u32[]{:S(2)}) collective-permute-start(bf16[128,1536]{1,0:T(8,128)(2,1)} %collective-permute-done.81), channel_id=1, source_target_pairs={{0,4},{2,6},{4,0},{6,2},{8,12},{10,14},{12,8},{14,10},{16,20},{18,... | collective-permute-start | bytes 1179656 | tf_op jit(solution)/shard_map/ppermute | solution.py:82
  172.3 38.4 %collective-permute-start.85 = (bf16[128,1536]{1,0:T(8,128)(2,1)}, bf16[128,1536]{1,0:T(8,128)(2,1)}, u32[]{:S(2)}, u32[]{:S(2)}) collective-permute-start(bf16[128,1536]{1,0:T(8,128)(2,1)} %collective-permute-done.81), channel_id=1, source_target_pairs={{0,8},{2,10},{4,12},{6,14},{8,16},{10,18},{12,20},{14,22},{16,24},... | collective-permute-start | bytes 1179656 | tf_op jit(solution)/shard_map/ppermute | solution.py:82
  197.2 20.2 %collective-permute-start.16 = (bf16[256,256]{1,0:T(8,128)(2,1)S(1)}, bf16[256,256]{1,0:T(8,128)(2,1)S(1)}, u32[]{:S(2)}, u32[]{:S(2)}) collective-permute-start(bf16[256,256]{1,0:T(8,128)(2,1)S(1)} %pad_maximum_fusion.10.refs_0_), channel_id=1, source_target_pairs={{0,2},{2,0},{4,6},{6,4},{8,10},{10,8},{12,14},{14,12},{16,18},{18,... | collective-permute-start | bytes 393224 | tf_op jit(solution)/shard_map/ppermute | solution.py:82
  217.4 15.6 %collective-permute-start.87 = (bf16[128,1536]{1,0:T(8,128)(2,1)}, bf16[128,1536]{1,0:T(8,128)(2,1)S(1)}, u32[]{:S(2)}, u32[]{:S(2)}) collective-permute-start(bf16[128,1536]{1,0:T(8,128)(2,1)} %collective-permute-done.85), channel_id=1, source_target_pairs={{0,4},{2,6},{4,0},{6,2},{8,12},{10,14},{12,8},{14,10},{16,20},{18,... | collective-permute-start | bytes 1179656 | tf_op jit(solution)/shard_map/ppermute | solution.py:82
  224.9 16.8 %collective-permute-start.84 = (bf16[128,1536]{1,0:T(8,128)(2,1)}, bf16[128,1536]{1,0:T(8,128)(2,1)S(1)}, u32[]{:S(2)}, u32[]{:S(2)}) collective-permute-start(bf16[128,1536]{1,0:T(8,128)(2,1)} %collective-permute-done.83), channel_id=1, source_target_pairs={{0,2},{2,0},{4,6},{6,4},{8,10},{10,8},{12,14},{14,12},{16,18},{18,... | collective-permute-start | bytes 1179656 | tf_op jit(solution)/shard_map/ppermute | solution.py:82
  233.0 126.0 %collective-permute-start.86 = (bf16[128,1536]{1,0:T(8,128)(2,1)}, bf16[128,1536]{1,0:T(8,128)(2,1)}, u32[]{:S(2)}, u32[]{:S(2)}) collective-permute-start(bf16[128,1536]{1,0:T(8,128)(2,1)} %collective-permute-done.85), channel_id=1, source_target_pairs={{0,2},{2,0},{4,6},{6,4},{8,10},{10,8},{12,14},{14,12},{16,18},{18,... | collective-permute-start | bytes 1179656 | tf_op jit(solution)/shard_map/ppermute | solution.py:82
  233.5 129.6 %collective-permute-start.88 = (bf16[128,1536]{1,0:T(8,128)(2,1)S(1)}, bf16[128,1536]{1,0:T(8,128)(2,1)}, u32[]{:S(2)}, u32[]{:S(2)}) collective-permute-start(bf16[128,1536]{1,0:T(8,128)(2,1)S(1)} %collective-permute-done.87), channel_id=1, source_target_pairs={{0,2},{2,0},{4,6},{6,4},{8,10},{10,8},{12,14},{14,12},{16,18},{18,... | collective-permute-start | bytes 1179656 | tf_op jit(solution)/shard_map/ppermute | solution.py:82
  257.2 14.4 %collective-permute-start.49 = (bf16[128,1664]{1,0:T(8,128)(2,1)S(1)}, bf16[128,1664]{1,0:T(8,128)(2,1)S(1)}, u32[]{:S(2)}, u32[]{:S(2)}) collective-permute-start(bf16[128,1664]{1,0:T(8,128)(2,1)S(1)} %concatenate.77), channel_id=1, source_target_pairs={{0,4},{2,6},{4,0},{6,2},{8,12},{10,14},{12,8},{14,10},{16,20},{18,... | collective-permute-start | bytes 1277960 | tf_op jit(solution)/shard_map/ppermute | solution.py:82
  261.6 35.1 %collective-permute-start.51 = (bf16[128,1664]{1,0:T(8,128)(2,1)S(1)}, bf16[128,1664]{1,0:T(8,128)(2,1)S(1)}, u32[]{:S(2)}, u32[]{:S(2)}) collective-permute-start(bf16[128,1664]{1,0:T(8,128)(2,1)S(1)} %concatenate.77), channel_id=1, source_target_pairs={{0,8},{2,10},{4,12},{6,14},{8,16},{10,18},{12,20},{14,22},{16,24},... | collective-permute-start | bytes 1277960 | tf_op jit(solution)/shard_map/ppermute | solution.py:82
  271.6 26.4 %collective-permute-start.50 = (bf16[128,1664]{1,0:T(8,128)(2,1)S(1)}, bf16[128,1664]{1,0:T(8,128)(2,1)S(1)}, u32[]{:S(2)}, u32[]{:S(2)}) collective-permute-start(bf16[128,1664]{1,0:T(8,128)(2,1)S(1)} %collective-permute-done.49), channel_id=1, source_target_pairs={{0,2},{2,0},{4,6},{6,4},{8,10},{10,8},{12,14},{14,12},{16,18},{18,... | collective-permute-start | bytes 1277960 | tf_op jit(solution)/shard_map/ppermute | solution.py:82
  298.0 13.8 %collective-permute-start.55 = (bf16[128,1664]{1,0:T(8,128)(2,1)S(1)}, bf16[128,1664]{1,0:T(8,128)(2,1)S(1)}, u32[]{:S(2)}, u32[]{:S(2)}) collective-permute-start(bf16[128,1664]{1,0:T(8,128)(2,1)S(1)} %collective-permute-done.51), channel_id=1, source_target_pairs={{0,8},{2,10},{4,12},{6,14},{8,16},{10,18},{12,20},{14,22},{16,24},... | collective-permute-start | bytes 1277960 | tf_op jit(solution)/shard_map/ppermute | solution.py:82
  311.8 16.9 %collective-permute-start.56 = (bf16[128,1664]{1,0:T(8,128)(2,1)S(1)}, bf16[128,1664]{1,0:T(8,128)(2,1)S(1)}, u32[]{:S(2)}, u32[]{:S(2)}) collective-permute-start(bf16[128,1664]{1,0:T(8,128)(2,1)S(1)} %collective-permute-done.55), channel_id=1, source_target_pairs={{0,2},{2,0},{4,6},{6,4},{8,10},{10,8},{12,14},{14,12},{16,18},{18,... | collective-permute-start | bytes 1277960 | tf_op jit(solution)/shard_map/ppermute | solution.py:82
  311.8 17.1 %collective-permute-start.57 = (bf16[128,1664]{1,0:T(8,128)(2,1)S(1)}, bf16[128,1664]{1,0:T(8,128)(2,1)S(1)}, u32[]{:S(2)}, u32[]{:S(2)}) collective-permute-start(bf16[128,1664]{1,0:T(8,128)(2,1)S(1)} %collective-permute-done.55), channel_id=1, source_target_pairs={{0,4},{2,6},{4,0},{6,2},{8,12},{10,14},{12,8},{14,10},{16,20},{18,... | collective-permute-start | bytes 1277960 | tf_op jit(solution)/shard_map/ppermute | solution.py:82
  313.8 28.4 %collective-permute-start.59 = (bf16[128,1664]{1,0:T(8,128)(2,1)S(1)}, bf16[128,1664]{1,0:T(8,128)(2,1)S(1)}, u32[]{:S(2)}, u32[]{:S(2)}) collective-permute-start(bf16[128,1664]{1,0:T(8,128)(2,1)S(1)} %collective-permute-done.55), channel_id=1, source_target_pairs={{0,8},{2,10},{4,12},{6,14},{8,16},{10,18},{12,20},{14,22},{16,24},... | collective-permute-start | bytes 1277960 | tf_op jit(solution)/shard_map/ppermute | solution.py:82
  329.0 13.8 %collective-permute-start.58 = (bf16[128,1664]{1,0:T(8,128)(2,1)S(1)}, bf16[128,1664]{1,0:T(8,128)(2,1)S(1)}, u32[]{:S(2)}, u32[]{:S(2)}) collective-permute-start(bf16[128,1664]{1,0:T(8,128)(2,1)S(1)} %collective-permute-done.57), channel_id=1, source_target_pairs={{0,2},{2,0},{4,6},{6,4},{8,10},{10,8},{12,14},{14,12},{16,18},{18,... | collective-permute-start | bytes 1277960 | tf_op jit(solution)/shard_map/ppermute | solution.py:82
  356.4 76.6 %collective-permute-start.138 = (bf16[16,2,32,1664]{3,2,0,1:T(8,128)(2,1)S(1)}, bf16[16,2,32,1664]{3,2,0,1:T(8,128)(2,1)S(1)}, u32[]{:S(2)}, u32[]{:S(2)}) collective-permute-start(bf16[16,2,32,1664]{3,2,0,1:T(8,128)(2,1)S(1)} %constant_dynamic-update-slice_fusion.16), channel_id=1, source_target_pairs={{0,1},{1,0},{2,3},{3,2},{4,5},{5,4},{6,7},{7,6},{8,9},{9,8},{10,11... | collective-permute-start | bytes 10223624 | tf_op jit(solution)/shard_map/ppermute | solution.py:117
  365.4 134.4 %collective-permute-start.139 = (bf16[16,64,1536]{2,1,0:T(8,128)(2,1)}, bf16[16,64,1536]{2,1,0:T(8,128)(2,1)}, u32[]{:S(2)}, u32[]{:S(2)}) collective-permute-start(bf16[16,64,1536]{2,1,0:T(8,128)(2,1)} %get-tuple-element.214), channel_id=1, source_target_pairs={{0,1},{1,0},{2,3},{3,2},{4,5},{5,4},{6,7},{7,6},{8,9},{9,8},{10,11... | collective-permute-start | bytes 9437192 | tf_op jit(solution)/shard_map/ppermute | solution.py:117
  479.3 63.4 %all-to-all-start = ((f32[16,2,128]{2,1,0:T(2,128)}), f32[16,2,128]{2,1,0:T(2,128)S(1)}, u32[]{:S(2)}, u32[]{:S(2)}) async-start(f32[16,2,128]{2,1,0:T(2,128)} %broadcast_select_fusion.4), calls=%async_computation | async-start | bytes 32768 | tf_op jit(solution)/shard_map/all_to_all | solution.py:445
  482.9 60.0 %collective-permute-start.95 = (bf16[2,128,1536]{2,1,0:T(8,128)(2,1)}, bf16[2,128,1536]{2,1,0:T(8,128)(2,1)}, u32[]{:S(2)}, u32[]{:S(2)}) collective-permute-start(bf16[2,128,1536]{2,1,0:T(8,128)(2,1)} %convolution_convert_fusion.2), channel_id=1, source_target_pairs={{0,2},{2,0},{4,6},{6,4},{8,10},{10,8},{12,14},{14,12},{16,18},{18,... | collective-permute-start | bytes 2359304 | tf_op jit(solution)/shard_map/ppermute | solution.py:82
  550.0 45.4 %collective-permute-start.94 = (bf16[128,1536]{1,0:T(8,128)(2,1)S(1)}, bf16[128,1536]{1,0:T(8,128)(2,1)S(1)}, u32[]{:S(2)}, u32[]{:S(2)}) collective-permute-start(bf16[128,1536]{1,0:T(8,128)(2,1)S(1)} %fusion.108), channel_id=1, source_target_pairs={{0,4},{2,6},{4,0},{6,2},{8,12},{10,14},{12,8},{14,10},{16,20},{18,... | collective-permute-start | bytes 1179656 | tf_op jit(solution)/shard_map/ppermute | solution.py:82
  552.9 63.5 %collective-permute-start.92 = (bf16[128,1536]{1,0:T(8,128)(2,1)S(1)}, bf16[128,1536]{1,0:T(8,128)(2,1)S(1)}, u32[]{:S(2)}, u32[]{:S(2)}) collective-permute-start(bf16[128,1536]{1,0:T(8,128)(2,1)S(1)} %fusion.107), channel_id=1, source_target_pairs={{0,4},{2,6},{4,0},{6,2},{8,12},{10,14},{12,8},{14,10},{16,20},{18,... | collective-permute-start | bytes 1179656 | tf_op jit(solution)/shard_map/ppermute | solution.py:82
  554.4 84.3 %collective-permute-start.90 = (bf16[128,1536]{1,0:T(8,128)(2,1)S(1)}, bf16[128,1536]{1,0:T(8,128)(2,1)S(1)}, u32[]{:S(2)}, u32[]{:S(2)}) collective-permute-start(bf16[128,1536]{1,0:T(8,128)(2,1)S(1)} %fusion.106), channel_id=1, source_target_pairs={{0,4},{2,6},{4,0},{6,2},{8,12},{10,14},{12,8},{14,10},{16,20},{18,... | collective-permute-start | bytes 1179656 | tf_op jit(solution)/shard_map/ppermute | solution.py:82
  556.2 38.0 %collective-permute-start.70 = (bf16[128,1536]{1,0:T(8,128)(2,1)S(1)}, bf16[128,1536]{1,0:T(8,128)(2,1)S(1)}, u32[]{:S(2)}, u32[]{:S(2)}) collective-permute-start(bf16[128,1536]{1,0:T(8,128)(2,1)S(1)} %fusion.105), channel_id=1, source_target_pairs={{0,4},{2,6},{4,0},{6,2},{8,12},{10,14},{12,8},{14,10},{16,20},{18,... | collective-permute-start | bytes 1179656 | tf_op jit(solution)/shard_map/ppermute | solution.py:82
  560.5 45.4 %collective-permute-start.68 = (bf16[128,1536]{1,0:T(8,128)(2,1)S(1)}, bf16[128,1536]{1,0:T(8,128)(2,1)S(1)}, u32[]{:S(2)}, u32[]{:S(2)}) collective-permute-start(bf16[128,1536]{1,0:T(8,128)(2,1)S(1)} %fusion.104), channel_id=1, source_target_pairs={{0,4},{2,6},{4,0},{6,2},{8,12},{10,14},{12,8},{14,10},{16,20},{18,... | collective-permute-start | bytes 1179656 | tf_op jit(solution)/shard_map/ppermute | solution.py:82
  595.4 35.0 %collective-permute-start.66 = (bf16[128,1536]{1,0:T(8,128)(2,1)S(1)}, bf16[128,1536]{1,0:T(8,128)(2,1)S(1)}, u32[]{:S(2)}, u32[]{:S(2)}) collective-permute-start(bf16[128,1536]{1,0:T(8,128)(2,1)S(1)} %fusion.103), channel_id=1, source_target_pairs={{0,4},{2,6},{4,0},{6,2},{8,12},{10,14},{12,8},{14,10},{16,20},{18,... | collective-permute-start | bytes 1179656 | tf_op jit(solution)/shard_map/ppermute | solution.py:82
  605.9 42.7 %collective-permute-start.64 = (bf16[128,1536]{1,0:T(8,128)(2,1)S(1)}, bf16[128,1536]{1,0:T(8,128)(2,1)S(1)}, u32[]{:S(2)}, u32[]{:S(2)}) collective-permute-start(bf16[128,1536]{1,0:T(8,128)(2,1)S(1)} %fusion.102), channel_id=1, source_target_pairs={{0,4},{2,6},{4,0},{6,2},{8,12},{10,14},{12,8},{14,10},{16,20},{18,... | collective-permute-start | bytes 1179656 | tf_op jit(solution)/shard_map/ppermute | solution.py:82
  616.2 13.8 %collective-permute-start.98 = (bf16[128,1536]{1,0:T(8,128)(2,1)S(1)}, bf16[128,1536]{1,0:T(8,128)(2,1)S(1)}, u32[]{:S(2)}, u32[]{:S(2)}) collective-permute-start(bf16[128,1536]{1,0:T(8,128)(2,1)S(1)} %fusion.74), channel_id=1, source_target_pairs={{0,8},{2,10},{4,12},{6,14},{8,16},{10,18},{12,20},{14,22},{16,24},... | collective-permute-start | bytes 1179656 | tf_op jit(solution)/shard_map/ppermute | solution.py:82
  616.4 22.0 %collective-permute-start.72 = (bf16[128,1536]{1,0:T(8,128)(2,1)S(1)}, bf16[128,1536]{1,0:T(8,128)(2,1)S(1)}, u32[]{:S(2)}, u32[]{:S(2)}) collective-permute-start(bf16[128,1536]{1,0:T(8,128)(2,1)S(1)} %fusion.81), channel_id=1, source_target_pairs={{0,8},{2,10},{4,12},{6,14},{8,16},{10,18},{12,20},{14,22},{16,24},... | collective-permute-start | bytes 1179656 | tf_op jit(solution)/shard_map/ppermute | solution.py:82
  630.3 16.5 %collective-permute-start.99 = (bf16[128,1536]{1,0:T(8,128)(2,1)S(1)}, bf16[128,1536]{1,0:T(8,128)(2,1)S(1)}, u32[]{:S(2)}, u32[]{:S(2)}) collective-permute-start(bf16[128,1536]{1,0:T(8,128)(2,1)S(1)} %fusion.76), channel_id=1, source_target_pairs={{0,8},{2,10},{4,12},{6,14},{8,16},{10,18},{12,20},{14,22},{16,24},... | collective-permute-start | bytes 1179656 | tf_op jit(solution)/shard_map/ppermute | solution.py:82
  685.9 19.9 %collective-permute-start.101 = (bf16[2,256,256]{2,1,0:T(8,128)(2,1)}, bf16[2,256,256]{2,1,0:T(8,128)(2,1)S(1)}, u32[]{:S(2)}, u32[]{:S(2)}) collective-permute-start(bf16[2,256,256]{2,1,0:T(8,128)(2,1)} %get-tuple-element.134), channel_id=1, source_target_pairs={{0,2},{2,0},{4,6},{6,4},{8,10},{10,8},{12,14},{14,12},{16,18},{18,... | collective-permute-start | bytes 786440 | tf_op jit(solution)/shard_map/ppermute | solution.py:82
  686.4 19.6 %collective-permute-start.105 = (bf16[2,256,256]{2,1,0:T(8,128)(2,1)}, bf16[2,256,256]{2,1,0:T(8,128)(2,1)}, u32[]{:S(2)}, u32[]{:S(2)}) collective-permute-start(bf16[2,256,256]{2,1,0:T(8,128)(2,1)} %get-tuple-element.137), channel_id=1, source_target_pairs={{0,2},{2,0},{4,6},{6,4},{8,10},{10,8},{12,14},{14,12},{16,18},{18,... | collective-permute-start | bytes 786440 | tf_op jit(solution)/shard_map/ppermute | solution.py:82
  686.5 19.9 %collective-permute-start.103 = (bf16[2,256,256]{2,1,0:T(8,128)(2,1)}, bf16[2,256,256]{2,1,0:T(8,128)(2,1)}, u32[]{:S(2)}, u32[]{:S(2)}) collective-permute-start(bf16[2,256,256]{2,1,0:T(8,128)(2,1)} %get-tuple-element.135), channel_id=1, source_target_pairs={{0,2},{2,0},{4,6},{6,4},{8,10},{10,8},{12,14},{14,12},{16,18},{18,... | collective-permute-start | bytes 786440 | tf_op jit(solution)/shard_map/ppermute | solution.py:82
  699.6 16.7 %collective-permute-start.131 = (bf16[2,48,1536]{2,1,0:T(8,128)(2,1)S(1)}, bf16[2,48,1536]{2,1,0:T(8,128)(2,1)S(1)}, u32[]{:S(2)}, u32[]{:S(2)}) collective-permute-start(bf16[2,48,1536]{2,1,0:T(8,128)(2,1)S(1)} %get-tuple-element.128), channel_id=1, source_target_pairs={{0,2},{2,0},{4,6},{6,4},{8,10},{10,8},{12,14},{14,12},{16,18},{18,... | collective-permute-start | bytes 884744 | tf_op jit(solution)/shard_map/ppermute | solution.py:82
  705.8 33.1 %collective-permute-start.125 = (bf16[2,48,1536]{2,1,0:T(8,128)(2,1)S(1)}, bf16[2,48,1536]{2,1,0:T(8,128)(2,1)S(1)}, u32[]{:S(2)}, u32[]{:S(2)}) collective-permute-start(bf16[2,48,1536]{2,1,0:T(8,128)(2,1)S(1)} %get-tuple-element.126), channel_id=1, source_target_pairs={{0,2},{2,0},{4,6},{6,4},{8,10},{10,8},{12,14},{14,12},{16,18},{18,... | collective-permute-start | bytes 884744 | tf_op jit(solution)/shard_map/ppermute | solution.py:82
  706.0 34.5 %collective-permute-start.129 = (bf16[2,48,1536]{2,1,0:T(8,128)(2,1)S(1)}, bf16[2,48,1536]{2,1,0:T(8,128)(2,1)S(1)}, u32[]{:S(2)}, u32[]{:S(2)}) collective-permute-start(bf16[2,48,1536]{2,1,0:T(8,128)(2,1)S(1)} %get-tuple-element.129), channel_id=1, source_target_pairs={{0,2},{2,0},{4,6},{6,4},{8,10},{10,8},{12,14},{14,12},{16,18},{18,... | collective-permute-start | bytes 884744 | tf_op jit(solution)/shard_map/ppermute | solution.py:82
  706.3 34.2 %collective-permute-start.127 = (bf16[2,48,1536]{2,1,0:T(8,128)(2,1)S(1)}, bf16[2,48,1536]{2,1,0:T(8,128)(2,1)S(1)}, u32[]{:S(2)}, u32[]{:S(2)}) collective-permute-start(bf16[2,48,1536]{2,1,0:T(8,128)(2,1)S(1)} %get-tuple-element.127), channel_id=1, source_target_pairs={{0,2},{2,0},{4,6},{6,4},{8,10},{10,8},{12,14},{14,12},{16,18},{18,... | collective-permute-start | bytes 884744 | tf_op jit(solution)/shard_map/ppermute | solution.py:82
  710.3 25.6 %collective-permute-start.109 = (bf16[256,256]{1,0:T(8,128)(2,1)S(1)}, bf16[256,256]{1,0:T(8,128)(2,1)S(1)}, u32[]{:S(2)}, u32[]{:S(2)}) collective-permute-start(bf16[256,256]{1,0:T(8,128)(2,1)S(1)} %get-tuple-element.131), channel_id=1, source_target_pairs={{0,8},{2,10},{4,12},{6,14},{8,16},{10,18},{12,20},{14,22},{16,24},... | collective-permute-start | bytes 393224 | tf_op jit(solution)/shard_map/ppermute | solution.py:82
  716.3 21.1 %collective-permute-start.106 = (bf16[256,256]{1,0:T(8,128)(2,1)S(1)}, bf16[256,256]{1,0:T(8,128)(2,1)S(1)}, u32[]{:S(2)}, u32[]{:S(2)}) collective-permute-start(bf16[256,256]{1,0:T(8,128)(2,1)S(1)} %get-tuple-element.132), channel_id=1, source_target_pairs={{0,4},{2,6},{4,0},{6,2},{8,12},{10,14},{12,8},{14,10},{16,20},{18,... | collective-permute-start | bytes 393224 | tf_op jit(solution)/shard_map/ppermute | solution.py:82
  745.5 32.2 %collective-permute-start.128 = (bf16[48,1536]{1,0:T(8,128)(2,1)}, bf16[48,1536]{1,0:T(8,128)(2,1)}, u32[]{:S(2)}, u32[]{:S(2)}) collective-permute-start(bf16[48,1536]{1,0:T(8,128)(2,1)} %get-tuple-element.125), channel_id=1, source_target_pairs={{0,4},{2,6},{4,0},{6,2},{8,12},{10,14},{12,8},{14,10},{16,20},{18,... | collective-permute-start | bytes 442376 | tf_op jit(solution)/shard_map/ppermute | solution.py:82
  747.6 35.8 %collective-permute-start.126 = (bf16[48,1536]{1,0:T(8,128)(2,1)}, bf16[48,1536]{1,0:T(8,128)(2,1)}, u32[]{:S(2)}, u32[]{:S(2)}) collective-permute-start(bf16[48,1536]{1,0:T(8,128)(2,1)} %get-tuple-element.122), channel_id=1, source_target_pairs={{0,4},{2,6},{4,0},{6,2},{8,12},{10,14},{12,8},{14,10},{16,20},{18,... | collective-permute-start | bytes 442376 | tf_op jit(solution)/shard_map/ppermute | solution.py:82
  752.2 25.6 %collective-permute-start.134 = (bf16[48,1536]{1,0:T(8,128)(2,1)}, bf16[48,1536]{1,0:T(8,128)(2,1)}, u32[]{:S(2)}, u32[]{:S(2)}) collective-permute-start(bf16[48,1536]{1,0:T(8,128)(2,1)} %fusion.122), channel_id=1, source_target_pairs={{0,8},{2,10},{4,12},{6,14},{8,16},{10,18},{12,20},{14,22},{16,24},... | collective-permute-start | bytes 442376 | tf_op jit(solution)/shard_map/ppermute | solution.py:82
  789.5 32.6 %collective-permute-start.136 = (bf16[48,1536]{1,0:T(8,128)(2,1)}, bf16[48,1536]{1,0:T(8,128)(2,1)}, u32[]{:S(2)}, u32[]{:S(2)}) collective-permute-start(bf16[48,1536]{1,0:T(8,128)(2,1)} %fusion.130), channel_id=1, source_target_pairs={{0,0},{2,1},{4,2},{6,3},{8,4},{10,5},{12,6},{14,7},{16,8},{18,9},{... | collective-permute-start | bytes 442376 | tf_op jit(solution)/shard_map/ppermute | solution.py:525
  792.3 33.8 %collective-permute-start.118 = (bf16[96,1152]{1,0:T(8,128)(2,1)}, bf16[96,1152]{1,0:T(8,128)(2,1)}, u32[]{:S(2)}, u32[]{:S(2)}) collective-permute-start(bf16[96,1152]{1,0:T(8,128)(2,1)} %get-tuple-element.116), channel_id=1, source_target_pairs={{0,4},{2,6},{4,0},{6,2},{8,12},{10,14},{12,8},{14,10},{16,20},{18,... | collective-permute-start | bytes 663560 | tf_op jit(solution)/shard_map/ppermute | solution.py:82
  793.1 33.0 %collective-permute-start.121 = (bf16[96,1152]{1,0:T(8,128)(2,1)S(1)}, bf16[96,1152]{1,0:T(8,128)(2,1)}, u32[]{:S(2)}, u32[]{:S(2)}) collective-permute-start(bf16[96,1152]{1,0:T(8,128)(2,1)S(1)} %fusion.89), channel_id=1, source_target_pairs={{0,8},{2,10},{4,12},{6,14},{8,16},{10,18},{12,20},{14,22},{16,24},... | collective-permute-start | bytes 663560 | tf_op jit(solution)/shard_map/ppermute | solution.py:82
  822.0 16.4 %collective-permute-start.112 = (bf16[128,1536]{1,0:T(8,128)(2,1)S(1)}, bf16[128,1536]{1,0:T(8,128)(2,1)S(1)}, u32[]{:S(2)}, u32[]{:S(2)}) collective-permute-start(bf16[128,1536]{1,0:T(8,128)(2,1)S(1)} %slice.1291), channel_id=1, source_target_pairs={{0,1},{1,0},{2,3},{3,2},{4,5},{5,4},{6,7},{7,6},{8,9},{9,8},{10,11... | collective-permute-start | bytes 1179656 | tf_op jit(solution)/shard_map/ppermute | solution.py:117
  822.1 14.4 %collective-permute-start.137 = (bf16[48,1536]{1,0:T(8,128)(2,1)}, bf16[48,1536]{1,0:T(8,128)(2,1)S(1)}, u32[]{:S(2)}, u32[]{:S(2)}) collective-permute-start(bf16[48,1536]{1,0:T(8,128)(2,1)} %collective-permute-done.136), channel_id=1, source_target_pairs={{0,1},{1,0},{2,3},{3,2},{4,5},{5,4},{6,7},{7,6},{8,9},{9,8},{10,11... | collective-permute-start | bytes 442376 | tf_op jit(solution)/shard_map/ppermute | solution.py:117
  824.1 16.3 %collective-permute-start.116 = (bf16[96,1152]{1,0:T(8,128)(2,1)}, bf16[96,1152]{1,0:T(8,128)(2,1)S(1)}, u32[]{:S(2)}, u32[]{:S(2)}) collective-permute-start(bf16[96,1152]{1,0:T(8,128)(2,1)} %get-tuple-element.117), channel_id=1, source_target_pairs={{0,4},{2,6},{4,0},{6,2},{8,12},{10,14},{12,8},{14,10},{16,20},{18,... | collective-permute-start | bytes 663560 | tf_op jit(solution)/shard_map/ppermute | solution.py:82
  (240 other events, 4403.9 us)
